TPU v7x, 32 devices: a whole 2x2x4 slice. The times are simulated.
32 devices in a mesh: dp: 4 (over y, x), seq: 8 (over z, core).
Axes of the slice: x: 2, y: 2, z: 4, core: 2. Of those that a mesh axis runs over, the one named last changes fastest.
Arguments:
- tokens: bfloat16 [32768, 512], P(('dp', 'seq')), may hold values from -6 to 6
- counts: int32 [4, 8], P('dp'), may hold values from 1 to 2048, 8192 in all within a row
- w_query: bfloat16 [512, 512], replicated, may hold values from -0.25 to 0.25
- b_query: float32 [512], replicated, may hold values from -3 to 3
- w_key: bfloat16 [512, 512], replicated, may hold values from -0.25 to 0.25
- w_value: bfloat16 [512, 512], replicated, may hold values from -0.25 to 0.25
- b_value: float32 [512], replicated, may hold values from -3 to 3
- w_out: bfloat16 [512, 512], replicated, may hold values from -3 to 3
- b_out: float32 [512], replicated, may hold values from -2 to 2
- gain_one: float32 [512], replicated, may hold values from 0.25 to 1.75
- shift_one: float32 [512], replicated, may hold values from -2 to 2
- w_up: bfloat16 [512, 1024], replicated, may hold values from -0.25 to 0.25
- b_up: float32 [1024], replicated, may hold values from -3 to 3
- w_down: bfloat16 [1024, 512], replicated, may hold values from -0.1875 to 0.1875
- b_down: float32 [512], replicated, may hold values from -2 to 2
- gain_two: float32 [512], replicated, may hold values from 0.25 to 1.75
- shift_two: float32 [512], replicated, may hold values from -2 to 2
- cotangent: bfloat16 [32768, 512], P(('dp', 'seq')), may hold values from -6 to 6
Outputs:
- layer_out: bfloat16 [32768, 512], P(('dp', 'seq'))
- input_grad: float32 [32768, 512], P(('dp', 'seq'))
- grad_w_query: float32 [512, 512], replicated
- grad_b_query: float32 [512], replicated
- grad_w_key: float32 [512, 512], replicated
- grad_w_value: float32 [512, 512], replicated
- grad_b_value: float32 [512], replicated
- grad_w_out: float32 [512, 512], replicated
- grad_b_out: float32 [512], replicated
- grad_gain_one: float32 [512], replicated
- grad_shift_one: float32 [512], replicated
- grad_w_up: float32 [512, 1024], replicated
- grad_b_up: float32 [1024], replicated
- grad_w_down: float32 [1024, 512], replicated
- grad_b_down: float32 [512], replicated
- grad_gain_two: float32 [512], replicated
- grad_shift_two: float32 [512], replicated
Inputs may be any that keep to these rules, and one draw needn't show every extreme that they name: counts[g] lists the samples of the 8 datasets of group g, laid end to end over the group's 8192 rows in the order of the devices of seq; they sum to 8192 and the largest is 2048.
All inputs are finite; a program needn't handle non-finite values.
Results may differ from a plain program's by a relative error of at most 0.023.
Values may be sent and summed in bfloat16 or wider, within the bound.
No kernel may reach another device: no remote copies, remote signals or barrier semaphores. Data moves between devices by JAX's collectives and lax.ppermute only.
A program may use at most 256 MiB of HBM per device.

v0:
```python
import functools
import math

import jax
import jax.numpy as jnp
from jax import lax
from jax.experimental import pallas as pl
from jax.experimental.pallas import tpu as pltpu
from jax.sharding import PartitionSpec as P

H = 4
HD = 128
EPS = 1e-05
BIG = 1e30
T = 256
LANES = 128
SCALE = 1.0 / math.sqrt(HD)
LOG2E = 1.0 / math.log(2.0)
LN2 = math.log(2.0)
F32 = jnp.float32
BF16 = jnp.bfloat16

NN = (((1,), (0,)), ((), ()))
NT = (((1,), (1,)), ((), ()))
TN = (((0,), (0,)), ((), ()))


def dot(left, right, dims=NN):
    return lax.dot_general(left, right, dims, preferred_element_type=F32)


def head(h):
    return slice(h * HD, (h + 1) * HD)


def query_mask(starts, ends, start):
    place = start + lax.broadcasted_iota(jnp.int32, (LANES, T), 1)
    inside = jnp.logical_and(place >= starts, place < ends)
    return jnp.where(inside, 1.0, 0.0).astype(BF16)


def key_mask(brow_ref, start):
    place = start + lax.broadcasted_iota(jnp.int32, (T, LANES), 0)
    inside = jnp.logical_and(place >= brow_ref[0:1, :], place < brow_ref[1:2, :])
    return jnp.where(inside, 0.0, -BIG).astype(BF16)


def tile_range(lo, hi, start, tiles):
    first = jnp.clip((lo - start) // T, 0, tiles)
    last = jnp.clip((hi - start + T - 1) // T, 0, tiles)
    return first, last


class Meta:
    def __init__(self, ref, nq):
        self.ref, self.nq = ref, nq
        self.chip, self.side, self.forward, self.own_tile, self.near_tile = (ref[2 * nq + j] for j in range(5))
        self.partner_tile = nq - self.own_tile
        self.far_tile = nq - self.near_tile
        self.own = self.chip + self.own_tile * T

    def lo(self, i):
        return self.ref[i]

    def hi(self, i):
        return self.ref[self.nq + i]

    @property
    def all_keys(self):
        return self.ref[0], self.ref[2 * self.nq - 1]


def survey(nq, seq, counts_ref, position_ref, meta_ref, brow_ref):
    position = position_ref[0]
    shard = nq * T
    sizes = [counts_ref[0, j] for j in range(counts_ref.shape[1])]
    starts, ends, end = [], [], 0
    for size in sizes:
        starts.append(end + 0 * size)
        end = end + size
        ends.append(end)
    for i in range(nq):
        first = position * shard + i * T
        lo, hi = 0, seq * shard
        for a, b in zip(starts[::-1], ends[::-1]):
            lo = jnp.maximum(lo, jnp.where(a <= first, a, 0))
            hi = jnp.minimum(hi, jnp.where(b > first + (T - 1), b, seq * shard))
        meta_ref[i] = lo
        meta_ref[nq + i] = hi
    core = position % 2
    side = position + jnp.where(core == 0, -2, 1)
    forward = position + jnp.where(core == 0, 2, -2)
    meta_ref[2 * nq] = (position - core) * shard
    meta_ref[2 * nq + 1] = jnp.where(jnp.logical_and(side >= 0, side + 1 < seq), side * shard, 1 << 28)
    meta_ref[2 * nq + 2] = jnp.where(jnp.logical_and(forward >= 0, forward < seq), forward * shard, 1 << 28)
    meta_ref[2 * nq + 3] = core * nq
    meta_ref[2 * nq + 4] = (1 - core) * nq

    def spread(values, shape, dimension):
        at = lax.broadcasted_iota(jnp.int32, shape, dimension)
        out = jnp.zeros(shape, jnp.int32)
        for j, value in enumerate(values):
            out = jnp.where(at == j, value, out)
        return out

    brow_ref[0:1, :] = spread(starts, (1, LANES), 1)
    brow_ref[1:2, :] = spread(ends, (1, LANES), 1)
    brow_ref[2:8, :] = jnp.zeros((6, LANES), jnp.int32)
    return spread(starts, (LANES, 1), 0), spread(ends, (LANES, 1), 0)


LIMIT_SQUARED = 9000.0


def head_pick(width):
    shape = (width, LANES)
    same = lax.broadcasted_iota(jnp.int32, shape, 0) // HD == lax.broadcasted_iota(jnp.int32, shape, 1)
    return jnp.where(same, 1.0, 0.0).astype(BF16)


def keep_norms(norm_ref, rows):
    squares = dot((rows * rows).astype(BF16), head_pick(rows.shape[1]))
    norm_ref[0:1, :] = jnp.maximum(norm_ref[0:1, :], jnp.max(squares, axis=0, keepdims=True))


def attend(meta, segments, qt_ref, k_ref, vt_ref, km_ref, qm_ref, acc_ref, top_ref, total_ref, safe, finish):
    nq = meta.nq

    def query_tile(i, carry):
        q0 = pl.multiple_of(i * T, T)
        qs = pl.ds(q0, T)

        def scores(h, k0):
            ks = pl.ds(k0, 2 * T)
            kx = jnp.concatenate([k_ref[ks, head(h)], km_ref[ks, :]], axis=1)
            qx = jnp.concatenate([qt_ref[head(h), qs], qm_ref[i]], axis=0)
            return dot(kx, qx)

        def weigh(h, k0, p):
            values = jnp.concatenate([vt_ref[head(h), pl.ds(k0, 2 * T)], jnp.ones((16, 2 * T), BF16)], axis=0)
            return dot(values, p)

        def plain(k0):
            ps = [jnp.exp2(scores(h, k0)).astype(BF16) for h in range(H)]
            sums = [weigh(h, k0, ps[h]) for h in range(H)]
            acc_ref[:, qs] += jnp.concatenate([out[0:HD] for out in sums], axis=0)
            for h in range(H):
                total_ref[h : h + 1, qs] += sums[h][HD : HD + 1]

        def guarded(k0):
            for h in range(H):
                s = scores(h, k0)
                old = top_ref[h : h + 1, qs]
                top = jnp.maximum(old, jnp.max(s, axis=0, keepdims=True))
                decay = jnp.exp2(old - top)
                out = weigh(h, k0, jnp.exp2(s - top).astype(BF16))
                acc_ref[head(h), qs] = acc_ref[head(h), qs] * decay + out[0:HD]
                total_ref[h : h + 1, qs] = total_ref[h : h + 1, qs] * decay + out[HD : HD + 1]
                top_ref[h : h + 1, qs] = top

        def walk(body):
            for start, tile, tiles in segments:
                first, last = tile_range(meta.lo(i), meta.hi(i), start, tiles)

                def step(j, inner):
                    body(pl.multiple_of((tile + first + 2 * j) * T, T))
                    return inner

                lax.fori_loop(0, (last - first + 1) // 2, step, 0)

        @pl.when(safe)
        def _():
            walk(plain)

        @pl.when(jnp.logical_not(safe))
        def _():
            walk(guarded)

        finish(q0)
        return carry

    lax.fori_loop(0, nq, query_tile, 0)


def project_keys(meta, brow_ref, start, tile, x_ref, wk_ref, wv_ref, bv_ref, k_ref, v_ref, vt_ref, km_ref, norm_ref):
    lo, hi = meta.all_keys
    first, last = tile_range(lo, hi + T, start, meta.nq)

    def step(t, carry):
        r0 = pl.multiple_of(t * T, T)
        ks = pl.ds(pl.multiple_of((tile + t) * T, T), T)
        x = x_ref[pl.ds(r0, T), :]
        k = dot(x, wk_ref[...])
        v = (dot(x, wv_ref[...]) + bv_ref[...]).astype(BF16)
        k_ref[ks, :] = k.astype(BF16)
        v_ref[ks, :] = v
        vt_ref[:, ks] = v.T
        km_ref[ks, :] = key_mask(brow_ref, start + r0)
        keep_norms(norm_ref, k)
        return carry

    lax.fori_loop(first, last, step, 0)


def blank_tile(tile, k_ref, vt_ref, km_ref):
    ks = slice(tile * T, (tile + 1) * T)
    k_ref[ks, :] = jnp.zeros((T, k_ref.shape[1]), BF16)
    vt_ref[:, ks] = jnp.zeros((vt_ref.shape[0], T), BF16)
    km_ref[ks, :] = jnp.full((T, LANES), -BIG, BF16)


def bounded(query_norms, key_norms):
    return jnp.max(query_norms * key_norms) <= LIMIT_SQUARED


def copies_of(sources, targets, sems):
    return [pltpu.make_async_copy(src, dst, sems.at[n]) for n, (src, dst) in enumerate(zip(sources, targets))]


def start(copies):
    for copy in copies:
        copy.start()


def wait(copies):
    for copy in copies:
        copy.wait()


def attend_chip_kernel(
    nq, seq,
    counts_ref, position_ref, bq_ref, bv_ref, xp_ref, *refs,
):
    sources, meta_ref, outs, held, refs = refs[:4], refs[4], refs[5:15], refs[15:25], refs[25:]
    q_ref, qt_ref, k_ref, v_ref, top_ref, total_ref, acc_ref, norm_ref, qm_ref, brow_ref = held
    vt_ref, km_ref, kn_ref, x_ref, wq_ref, wk_ref, wv_ref, sems, out_sems = refs
    loads = copies_of(sources, (x_ref, wq_ref, wk_ref, wv_ref), sems)
    stores = copies_of(held, outs, out_sems)
    start(loads[:2])
    starts, ends = survey(nq, seq, counts_ref, position_ref, meta_ref, brow_ref)
    meta = Meta(meta_ref, nq)
    wait(loads[:2])
    start(loads[2:])
    norm_ref[...] = jnp.zeros_like(norm_ref)
    kn_ref[...] = jnp.zeros_like(kn_ref)

    def make_query(i, carry):
        q0 = pl.multiple_of(i * T, T)
        q = (dot(x_ref[pl.ds(q0, T), :], wq_ref[...]) + bq_ref[...]) * (SCALE * LOG2E)
        low = q.astype(BF16)
        q_ref[pl.ds(q0, T), :] = low
        qt_ref[:, pl.ds(q0, T)] = low.T
        qm_ref[i] = query_mask(starts, ends, meta.own + q0)
        keep_norms(norm_ref, q)
        return carry

    lax.fori_loop(0, nq, make_query, 0)
    start(stores[:2] + stores[8:])
    wait(loads[2:])
    for rows, tile in ((x_ref, meta.own_tile), (xp_ref, meta.partner_tile)):
        project_keys(
            meta, brow_ref, meta.chip + tile * T, tile, rows, wk_ref, wv_ref, bv_ref,
            k_ref, v_ref, vt_ref, km_ref, kn_ref,
        )
    blank_tile(2 * nq, k_ref, vt_ref, km_ref)
    start(stores[2:4])
    acc_ref[...] = jnp.zeros_like(acc_ref)
    total_ref[...] = jnp.zeros_like(total_ref)
    safe = bounded(norm_ref[0:1, :], kn_ref[0:1, :])
    norm_ref[1:2, :] = jnp.full((1, LANES), jnp.where(safe, 1.0, 0.0), F32)
    top_ref[...] = jnp.full(top_ref.shape, jnp.where(safe, 0.0, -BIG), F32)
    attend(
        meta, [(meta.chip, 0, 2 * nq)], qt_ref, k_ref, vt_ref, km_ref, qm_ref, acc_ref, top_ref, total_ref, safe,
        lambda q0: None,
    )
    start(stores[4:8])
    wait(stores)


def attend_far(meta, brow_ref, blocks, queries, others, wk_ref, wv_ref, bv_ref, qt_ref, norm_ref, qm_ref,
               k_ref, v_ref, att_ref, attt_ref, lse_ref, vt_ref, km_ref, kn_ref, top_ref, total_ref):
    nq = meta.nq
    kn_ref[...] = jnp.zeros_like(kn_ref)
    for copies, rows, first_row, tile in blocks:
        wait(copies)
        project_keys(
            meta, brow_ref, first_row, tile, rows, wk_ref, wv_ref, bv_ref, k_ref, v_ref, vt_ref, km_ref, kn_ref
        )
    blank_tile(2 * nq, k_ref, vt_ref, km_ref)
    blank_tile(3 * nq + 1, k_ref, vt_ref, km_ref)
    wait(queries)
    start(others)

    def finish(q0):
        qs = pl.ds(q0, T)
        for h in range(H):
            total = total_ref[h : h + 1, qs]
            lse_ref[h : h + 1, qs] = top_ref[h : h + 1, qs] + jnp.log2(total)
            att = attt_ref[head(h), qs] / total
            attt_ref[head(h), qs] = att
            att_ref[qs, head(h)] = att.T.astype(BF16)

    safe = jnp.logical_and(bounded(norm_ref[0:1, :], kn_ref[0:1, :]), jnp.max(norm_ref[1:2, :]) > 0.5)
    attend(
        meta, [(meta.side, 0, 2 * nq), (meta.forward, 2 * nq + 1, nq)], qt_ref, k_ref, vt_ref, km_ref, qm_ref,
        attt_ref, top_ref, total_ref, safe, finish,
    )


def column_sum(rows):
    return jnp.sum(rows, axis=0, keepdims=True)


def mean(rows):
    return jnp.mean(rows, axis=-1, keepdims=True)


def norm(rows):
    centre = rows - mean(rows)
    inverse = lax.rsqrt(mean(centre * centre) + EPS)
    return centre * inverse, inverse


def norm_back(grad, n, inverse):
    return inverse * (grad - mean(grad) - n * mean(grad * n))


def middle(
    nq, x_ref, cot_ref, att_ref, attt_ref, wo_ref, wu_ref, wd_ref, vectors, bup_ref,
    dfirst_ref, da_ref, dat_ref, delta_ref, small_ref, gd_ref, gu_ref, go_ref,
):
    width = x_ref.shape[1]
    hidden = wu_ref.shape[1]
    b_out, gain_one, shift_one, b_down, gain_two, shift_two = (ref[...] for ref in vectors)
    for ref in (gd_ref, gu_ref, go_ref, small_ref):
        ref[...] = jnp.zeros_like(ref)
    rows_of = lambda tiles: jnp.concatenate(tiles, axis=0)

    def row_tiles(i, carry):
        both = [pl.ds(pl.multiple_of((2 * i + n) * T, T), T) for n in range(2)]
        att = [att_ref[rs, :] for rs in both]
        branch = [dot(a, wo_ref[...]) for a in att]
        one = [norm(x_ref[rs, :].astype(F32) + b + b_out) for rs, b in zip(both, branch)]
        normed = [n * gain_one + shift_one for n, _ in one]
        normed_low = [n.astype(BF16) for n in normed]
        pre, act_low, slope = [], [], []
        for n in range(2):
            pre.append(dot(normed_low[n], wu_ref[...]) + bup_ref[...])
        for n in range(2):
            cdf = 0.5 * (1.0 + lax.erf(pre[n] * math.sqrt(0.5)))
            act_low.append((pre[n] * cdf).astype(BF16))
            slope.append(cdf + pre[n] * (jnp.exp(-0.5 * pre[n] * pre[n]) * (1.0 / math.sqrt(2.0 * math.pi))))
        down = [dot(act, wd_ref[...]) for act in act_low]
        two = [norm(n + d + b_down) for n, d in zip(normed, down)]
        cot = [cot_ref[rs, :].astype(F32) for rs in both]
        for rs, (n, _) in zip(both, two):
            cot_ref[rs, :] = (n * gain_two + shift_two).astype(BF16)
        d_sum = [norm_back(c * gain_two, n, inverse) for c, (n, inverse) in zip(cot, two)]
        d_ffn = [d.astype(BF16) for d in d_sum]
        d_act = [dot(d, wd_ref[...], NT) for d in d_ffn]
        gd_ref[...] += dot(rows_of(act_low), rows_of(d_ffn), TN)
        d_pre = [(d * s).astype(BF16) for d, s in zip(d_act, slope)]
        d_normed = [a + dot(d, wu_ref[...], NT) for a, d in zip(d_sum, d_pre)]
        gu_ref[...] += dot(rows_of(normed_low), rows_of(d_pre), TN)
        d_first = [norm_back(d * gain_one, n, inverse) for d, (n, inverse) in zip(d_normed, one)]
        d_branch = [d.astype(BF16) for d in d_first]
        d_att = [dot(d, wo_ref[...], NT).astype(BF16) for d in d_branch]
        go_ref[...] += dot(rows_of(att), rows_of(d_branch), TN)
        for rs, d, a in zip(both, d_first, d_att):
            dfirst_ref[rs, :] = d
            da_ref[rs, :] = a
            turned = a.T
            dat_ref[:, rs] = turned
            for h in range(H):
                delta_ref[h : h + 1, rs] = column_sum(turned[head(h), :].astype(F32) * attt_ref[head(h), rs])
        pair_sum = lambda rows: column_sum(rows[0].astype(F32) + rows[1].astype(F32))
        up = pair_sum(d_pre)
        sums = [
            pair_sum(d_branch),
            pair_sum([d * n for d, (n, _) in zip(d_normed, one)]),
            pair_sum(d_normed),
            pair_sum(d_ffn),
            pair_sum([c * n for c, (n, _) in zip(cot, two)]),
            pair_sum(cot),
        ]
        for at in range(0, hidden, width):
            sums.append(up[:, at : at + width])
        small_ref[...] += jnp.concatenate(sums, axis=0)
        return carry

    lax.fori_loop(0, nq // 2, row_tiles, 0)


def attend_back(
    meta, brow_ref, start, tile, k_ref, v_ref, q_ref, qt_ref, da_ref, dat_ref, lse_ref, delta_ref, qm_ref,
    kt_ref, km_ref, dk_ref, dv_ref, dq_ref,
):
    nq = meta.nq
    first, last = tile_range(*meta.all_keys, start, nq)

    def rows_at(t):
        return pl.ds(pl.multiple_of((tile + t) * T, T), T)

    def blank(t, carry):
        for ref in (k_ref, v_ref):
            ref[rows_at(t), :] = jnp.zeros((T, ref.shape[1]), BF16)
        return carry

    def key_tile(t, carry):
        ks = rows_at(t)
        row = start + t * T
        q_first = sum((meta.hi(i) <= row).astype(jnp.int32) for i in range(nq))
        q_last = sum((meta.lo(i) < row + T).astype(jnp.int32) for i in range(nq))
        km_ref[...] = key_mask(brow_ref, row)
        kt_ref[...] = k_ref[ks, :].T
        dk_ref[...] = jnp.zeros_like(dk_ref)
        dv_ref[...] = jnp.zeros_like(dv_ref)

        def query_tile(i, inner):
            qs = pl.ds(pl.multiple_of(i * T, T), T)
            ps, ds, sums = [], [], []

            def products(h):
                sums.append((dot(ps[h], da_ref[qs, head(h)]), dot(ds[h], q_ref[qs, head(h)]), dot(kt_ref[head(h), :], ds[h])))

            for h in range(H):
                kx = jnp.concatenate([k_ref[ks, head(h)], km_ref[...]], axis=1)
                qx = jnp.concatenate([qt_ref[head(h), qs], qm_ref[i]], axis=0)
                p = jnp.exp2(dot(kx, qx) - lse_ref[h : h + 1, qs])
                ps.append(p.astype(BF16))
                dp = dot(v_ref[ks, head(h)], dat_ref[head(h), qs])
                ds.append((p * (dp - delta_ref[h : h + 1, qs])).astype(BF16))
                if h >= 2:
                    products(h - 2)
            products(H - 2)
            products(H - 1)
            dv_ref[...] += jnp.concatenate([out[0] for out in sums], axis=1)
            dk_ref[...] += jnp.concatenate([out[1] for out in sums], axis=1)
            dq_ref[:, qs] += jnp.concatenate([out[2] for out in sums], axis=0)
            return inner

        lax.fori_loop(q_first, q_last, query_tile, 0)
        k_ref[ks, :] = (dk_ref[...] * LN2).astype(BF16)
        v_ref[ks, :] = dv_ref[...].astype(BF16)
        return carry

    lax.fori_loop(0, first, blank, 0)
    lax.fori_loop(first, last, key_tile, 0)
    lax.fori_loop(last, nq, blank, 0)


def layer_kernel(
    nq,
    meta_ref, brow_ref, bv_ref, bup_ref, norm_ref, qm_ref, xw_ref, *refs,
):
    vectors, refs = refs[:6], refs[6:]
    count = 18
    sources, refs = refs[:count], refs[count:]
    layer_out, ig_out, pn_out, pf_out, pw_out, pp_out, keep_out, send_out = refs[:8]
    refs = refs[8:]
    staged, refs = refs[:count], refs[count:]
    sems, out_sems, grads_ref, ig_ref, k_ref, v_ref, vt_ref, km_ref, kn_ref, lse_ref, delta_ref, small_ref = refs[:12]
    att_ref, da_ref, dat_ref, gd_ref, gu_ref, go_ref, sum_ref = refs[12:19]
    kt_ref, mask_ref, dk_ref, dv_ref = refs[19:]
    loads = copies_of(sources, staged, sems)
    start(loads[:4])
    wk_ref, wv_ref, xn_ref, xf_ref, qt_ref, top_ref, total_ref, attt_ref = staged[:8]
    wo_ref, x_ref, wu_ref, wd_ref, cot_ref, q_ref, kc_ref, vc_ref, xp_ref, wq_ref = staged[8:]
    stores = []

    def store(source, target):
        copy = pltpu.make_async_copy(source, target, out_sems.at[len(stores)])
        copy.start()
        stores.append(copy)

    meta = Meta(meta_ref, nq)
    near_start = meta.side + meta.near_tile * T
    far_start = meta.side + meta.far_tile * T
    wait(loads[:2])
    start(loads[4:8])
    attend_far(
        meta, brow_ref,
        (
            ([], xw_ref, meta.forward, 2 * nq + 1),
            (loads[2:3], xn_ref, near_start, meta.near_tile),
            (loads[3:4], xf_ref, far_start, meta.far_tile),
        ),
        loads[4:8],
        loads[8:],
        wk_ref, wv_ref, bv_ref, qt_ref, norm_ref, qm_ref,
        k_ref, v_ref, att_ref, attt_ref, lse_ref, vt_ref, km_ref, kn_ref, top_ref, total_ref,
    )
    wait(loads[8:13])
    middle(
        nq, x_ref, cot_ref, att_ref, attt_ref, wo_ref, wu_ref, wd_ref, vectors, bup_ref,
        ig_ref, da_ref, dat_ref, delta_ref, small_ref, gd_ref, gu_ref, go_ref,
    )
    store(cot_ref, layer_out)
    hidden, width = wd_ref.shape
    shard = x_ref.shape[0]
    grads_ref[0:hidden, :] = gd_ref[...].astype(BF16)
    for part in range(hidden // width):
        at = hidden + part * width
        grads_ref[at : at + width, :] = gu_ref[:, part * width : (part + 1) * width].astype(BF16)
    base = 2 * hidden + width
    grads_ref[base - width : base, :] = go_ref[...].astype(BF16)
    half = grads_ref.shape[0] // 2
    assert half <= base
    first_core = meta.own_tile == 0

    def store_half(source, stays):
        copies = [pltpu.make_async_copy(source, target, out_sems.at[len(stores)]) for target in (keep_out, send_out)]
        pl.when(stays)(copies[0].start)
        pl.when(jnp.logical_not(stays))(copies[1].start)
        stores.append(copies[0])

    store_half(grads_ref.at[0:half, :], first_core)

    wait(loads[13:])
    xt_ref = vt_ref.at[:, 0:shard]
    dq_ref = attt_ref
    dwk_ref = gd_ref.at[0:width, :]
    dwv_ref = gd_ref.at[width : 2 * width, :]
    wkv_ref = wd_ref
    wkv_ref[0:width, :] = wk_ref[...].T
    wkv_ref[width : 2 * width, :] = wv_ref[...].T
    wo_ref[...] = wq_ref[...].T
    for ref in (dq_ref, dwk_ref, dwv_ref, sum_ref):
        ref[...] = jnp.zeros_like(ref)
    for rows, part_ref, out, first_row, tile, keys_ref, values_ref in (
        (xn_ref, xn_ref, pn_out, near_start, meta.near_tile, k_ref, v_ref),
        (xf_ref, xf_ref, pf_out, far_start, meta.far_tile, k_ref, v_ref),
        (xw_ref, att_ref, pw_out, meta.forward, 2 * nq + 1, k_ref, v_ref),
        (xp_ref, xp_ref, pp_out, meta.chip + meta.partner_tile * T, meta.partner_tile, kc_ref, vc_ref),
        (x_ref, None, None, meta.own, meta.own_tile, kc_ref, vc_ref),
    ):
        first, last = tile_range(*meta.all_keys, first_row, nq)

        def work(rows=rows, part_ref=part_ref, out=out, first_row=first_row, tile=tile, keys_ref=keys_ref, values_ref=values_ref):
            attend_back(
                meta, brow_ref, first_row, tile, keys_ref, values_ref, q_ref, qt_ref, da_ref, dat_ref,
                lse_ref, delta_ref, qm_ref, kt_ref, mask_ref, dk_ref, dv_ref, dq_ref,
            )
            block = pl.ds(pl.multiple_of(tile * T, T), shard)
            xt_ref[...] = rows[...].T
            dwk_ref[...] += dot(xt_ref[...], keys_ref[block, :])
            dwv_ref[...] += dot(xt_ref[...], values_ref[block, :])
            sum_ref[0:1, :] += column_sum(values_ref[block, :].astype(F32))

            def input_tile(t, carry):
                rs = pl.ds(pl.multiple_of(2 * t * T, 2 * T), 2 * T)
                ks = pl.ds(pl.multiple_of((tile + 2 * t) * T, T), 2 * T)
                grad = dot(jnp.concatenate([keys_ref[ks, :], values_ref[ks, :]], axis=1), wkv_ref[...])
                if out is None:
                    ig_ref[rs, :] += grad
                else:
                    part_ref[rs, :] = grad.astype(BF16)
                return carry

            lax.fori_loop(0, nq // 2, input_tile, 0)

        if out is None:
            work()
        else:
            pl.when(first < last)(work)

            @pl.when(first >= last)
            def _(part_ref=part_ref):
                part_ref[...] = jnp.zeros_like(part_ref)

            store(part_ref, out)

    dwk_low = dwk_ref[...].astype(BF16)
    dwv_low = dwv_ref[...].astype(BF16)

    def query_tile(i, carry):
        qs = pl.ds(pl.multiple_of(i * T, T), T)
        dq = (dq_ref[:, qs] * SCALE).astype(BF16).T
        q_ref[qs, :] = dq
        sum_ref[1:2, :] += column_sum(dq.astype(F32))
        ig_ref[qs, :] += dot(dq, wo_ref[...])
        return carry

    lax.fori_loop(0, nq, query_tile, 0)
    store(ig_ref, ig_out)
    grads_ref[base : base + width, :] = dot(xt_ref[...], q_ref[...]).astype(BF16)
    grads_ref[base + width : base + 2 * width, :] = dwk_low
    grads_ref[base + 2 * width : base + 3 * width, :] = dwv_low
    end = base + 3 * width
    rows = jnp.concatenate([sum_ref[...], small_ref[...]], axis=0)
    grads_ref[end : end + 16, :] = rows.astype(BF16)
    grads_ref[end + 16 :, :] = jnp.zeros((grads_ref.shape[0] - end - 16, width), BF16)
    store_half(grads_ref.at[half:, :], jnp.logical_not(first_core))
    wait(stores)


def vmem(count):
    return [pl.BlockSpec(memory_space=pltpu.VMEM)] * count


VMEM_LIMIT = 60 << 20


def call(kernel, inputs, staged, outputs, scratch, flops, scalars=1, out_scalars=0, limit=VMEM_LIMIT):
    size = lambda arrays: sum(math.prod(a.shape) * jnp.dtype(a.dtype).itemsize for a in arrays)
    everything = tuple(inputs) + tuple(staged)
    smem = [pl.BlockSpec(memory_space=pltpu.SMEM)]
    hbm = [pl.BlockSpec(memory_space=pltpu.HBM)]
    return pl.pallas_call(
        kernel,
        out_shape=outputs,
        in_specs=smem * scalars + vmem(len(inputs) - scalars) + hbm * len(staged),
        out_specs=smem * out_scalars + hbm * (len(outputs) - out_scalars),
        scratch_shapes=scratch,
        compiler_params=pltpu.CompilerParams(vmem_limit_bytes=limit),
        cost_estimate=pl.CostEstimate(
            flops=flops, bytes_accessed=size(everything) + size(outputs), transcendentals=0
        ),
    )(*everything)


def struct(shape, dtype):
    return jax.ShapeDtypeStruct(shape, dtype)


def after(value, other):
    return lax.optimization_barrier((value, other))[0]


class Summing:
    def __init__(self, dp, seq):
        dp_masks = [seq * (1 << j) for j in range(dp.bit_length() - 1)]
        seq_masks = [1 << j for j in range(seq.bit_length() - 1)]
        self.order = [(dp_masks[j], dp_masks[(j + 1) % len(dp_masks)]) for j in range(len(dp_masks))]
        self.dp_steps = len(self.order)
        self.order += [(mask, mask) for mask in seq_masks[1:]]
        self.devices = dp * seq
        core = lax.axis_index("seq") % 2
        index = lax.axis_index("dp") * seq + lax.axis_index("seq")
        self.bits = [jnp.where(core == 0, index // even, index // odd) % 2 for even, odd in self.order]

    def exchange(self, rows, even=1, odd=1):
        pairs = [(i, i ^ (even if i % 2 == 0 else odd)) for i in range(self.devices)]
        return lax.ppermute(rows, ("dp", "seq"), pairs)

    def halve(self, rows, number, other=None):
        half = rows.shape[0] // 2
        bit = self.bits[number]
        mine = lax.dynamic_slice_in_dim(rows, bit * half, half, 0)
        got = self.exchange(lax.dynamic_slice_in_dim(rows, (1 - bit) * half, half, 0), *self.order[number])
        return (mine if other is None else after(mine, other)) + got

    def whole(self, rows):
        return rows + self.exchange(rows, *self.order[-1])

    def double(self, rows, number, other=None):
        got = self.exchange(rows, *self.order[number])
        half = rows.shape[0]
        if other is not None:
            rows = after(rows, other)
        both = jnp.zeros((2 * half, rows.shape[1]), rows.dtype)
        both = lax.dynamic_update_slice_in_dim(both, rows, self.bits[number] * half, 0)
        return lax.dynamic_update_slice_in_dim(both, got, (1 - self.bits[number]) * half, 0)


def widen_kernel(bias_rows, core_ref, mine_one, mine_two, other_one, other_two, *refs):
    count = 6 + len(bias_rows)
    outs, wide, sems = refs[:count], refs[count : 2 * count], refs[2 * count]
    width = mine_one.shape[1]
    hidden = wide[0].shape[0]
    spans = [(0, hidden, 0, 0)]
    spans += [(hidden + at, width, 1, at) for at in range(0, hidden, width)]
    spans += [(2 * hidden + n * width, width, 2 + n, 0) for n in range(4)]
    copies = copies_of(wide, outs, sems)

    def write(*sources):
        bases = [sum(ref.shape[0] for ref in sources[:n]) for n in range(4)]
        for first_row, rows, number, column in spans:
            for source, base in zip(sources, bases):
                first, last = max(first_row, base), min(first_row + rows, base + source.shape[0])
                if first < last:
                    wide[number][first - first_row : last - first_row, column : column + width] = source[
                        first - base : last - base, :
                    ].astype(F32)
            if column + width == wide[number].shape[1]:
                copies[number].start()
        at = 2 * hidden + 4 * width - bases[3]
        vectors = sources[3][at : at + 16, :].astype(F32)
        for number, rows in enumerate(bias_rows):
            for part, row in enumerate(rows):
                wide[6 + number][:, part * width : (part + 1) * width] = vectors[row : row + 1, :]
            copies[6 + number].start()

    @pl.when(core_ref[0] == 0)
    def _():
        write(mine_one, mine_two, other_one, other_two)

    @pl.when(core_ref[0] != 0)
    def _():
        write(other_one, other_two, mine_one, mine_two)

    wait(copies)


def shards(
    tokens, counts, w_query, b_query, w_key, w_value, b_value, w_out, b_out, gain_one, shift_one,
    w_up, b_up, w_down, b_down, gain_two, shift_two, cotangent,
):
    shard, width = tokens.shape
    hidden = w_up.shape[1]
    nq = shard // T
    seq = lax.axis_size("seq")
    dp = lax.axis_size("dp")
    position = lax.axis_index("seq")

    def swap(rows):
        return lax.ppermute(rows, "seq", [(i, i ^ 1) for i in range(seq)])

    def near(rows):
        pairs = [(i, i + 1) for i in range(1, seq - 1, 2)]
        return lax.ppermute(rows, "seq", pairs + [(b, a) for a, b in pairs])

    def far(rows, back=False):
        pairs = [(i, i + 2) for i in range(0, seq - 2, 2)] + [(i, i - 2) for i in range(3, seq, 2)]
        return lax.ppermute(rows, "seq", [(b, a) for a, b in pairs] if back else pairs)

    x_partner = swap(tokens)
    x_near = near(tokens)
    x_far = far(tokens)

    core = position % 2
    row = lambda v: v.reshape(1, -1)
    tile_mask = struct((nq, LANES, T), BF16)
    stats = struct((8, shard), F32)

    def keys_scratch(tiles):
        return [
            pltpu.VMEM((width, tiles * T), BF16), pltpu.VMEM((tiles * T, LANES), BF16), pltpu.VMEM((8, LANES), F32)
        ]

    unit = 2 * shard * width * width
    chip_tiles, far_tiles = 2 * nq + 1, 3 * nq + 2
    keys = lambda tiles: struct((tiles * T, width), BF16)
    block = pltpu.VMEM((shard, width), BF16)
    weight = pltpu.VMEM((width, width), BF16)
    wide = pltpu.VMEM((width, shard), F32)
    square = pltpu.VMEM((width, width), F32)
    stat = pltpu.VMEM((8, shard), F32)
    part = struct((shard, width), BF16)
    meta, q, qt, k_chip, v_chip, top, total, acc, norms, qm, bounds = call(
        functools.partial(attend_chip_kernel, nq, seq),
        (counts, position.reshape(1).astype(jnp.int32), row(b_query), row(b_value), x_partner),
        (tokens, w_query, w_key, w_value),
        (
            struct((2 * nq + 5,), jnp.int32),
            part, struct((width, shard), BF16), keys(chip_tiles), keys(chip_tiles), stats, stats,
            struct((width, shard), F32), struct((8, LANES), F32), tile_mask, struct((8, LANES), jnp.int32),
        ),
        [
            block, pltpu.VMEM((width, shard), BF16), pltpu.VMEM((chip_tiles * T, width), BF16),
            pltpu.VMEM((chip_tiles * T, width), BF16), stat, stat, wide, pltpu.VMEM((8, LANES), F32),
            pltpu.VMEM((nq, LANES, T), BF16), pltpu.VMEM((8, LANES), jnp.int32),
        ]
        + keys_scratch(chip_tiles)
        + [block, weight, weight, weight, pltpu.SemaphoreType.DMA((4,)), pltpu.SemaphoreType.DMA((10,))],
        13 * unit,
        scalars=2,
        out_scalars=1,
    )
    x_forward = swap(after(x_near, norms))

    granule = 8 * dp * seq // 2
    grad_rows = (2 * hidden + 4 * width + 16 + granule - 1) // granule * granule
    vectors = [row(v) for v in (b_out, gain_one, shift_one, b_down, gain_two, shift_two)]
    layer, input_grad, p_near, p_far, p_forward, p_partner, keep, send = call(
        functools.partial(layer_kernel, nq),
        (meta, bounds, row(b_value), row(b_up), norms, qm, x_forward, *vectors),
        (
            w_key, w_value, x_near, x_far, qt, top, total, acc,
            w_out, tokens, w_up, w_down, cotangent, q, k_chip, v_chip, x_partner, w_query,
        ),
        (
            part, struct((shard, width), F32), part, part, part, part,
            struct((grad_rows // 2, width), BF16), struct((grad_rows // 2, width), BF16),
        ),
        [
            weight, weight, block, block, pltpu.VMEM((width, shard), BF16), stat, stat, wide,
            weight, block, pltpu.VMEM((width, hidden), BF16), pltpu.VMEM((hidden, width), BF16), block, block,
            pltpu.VMEM((chip_tiles * T, width), BF16), pltpu.VMEM((chip_tiles * T, width), BF16), block, weight,
            pltpu.SemaphoreType.DMA((18,)), pltpu.SemaphoreType.DMA((8,)),
            pltpu.VMEM((grad_rows, width), BF16), pltpu.VMEM((shard, width), F32),
            pltpu.VMEM((far_tiles * T, width), BF16), pltpu.VMEM((far_tiles * T, width), BF16),
        ]
        + keys_scratch(far_tiles)
        + [stat, stat, pltpu.VMEM((8, width), F32)]
        + [block, block, pltpu.VMEM((width, shard), BF16)]
        + [pltpu.VMEM((hidden, width), F32), pltpu.VMEM((width, hidden), F32), square]
        + [pltpu.VMEM((8, width), F32)]
        + [
            pltpu.VMEM((width, T), BF16), pltpu.VMEM((T, LANES), BF16),
            pltpu.VMEM((T, width), F32), pltpu.VMEM((T, width), F32),
        ],
        60 * unit,
    )
    summing = Summing(dp, seq)
    p_forward = swap(p_forward)
    grads = keep + summing.exchange(send)
    p_far = far(after(p_far, grads), back=True)
    p_partner = swap(after(p_partner, grads))
    p_near = p_near + p_forward
    unit = 8 << (len(summing.order) - 1)
    lead = (grad_rows // 2 // unit + 1) // 2 * unit
    one, two = grads[:lead], grads[lead:]
    dp_steps = summing.dp_steps
    steps = list(range(len(summing.order) - 1))
    others = {0: p_near, 1: p_partner, dp_steps: p_far}
    for number in steps:
        one = summing.halve(one, number, others.get(number))
        if number == 0:
            two = after(two, one)
    for number in steps:
        two = summing.halve(two, number)
    one, two = summing.whole(one), summing.whole(two)
    for number in steps[dp_steps:][::-1]:
        one, two = summing.double(one, number), summing.double(two, number)
    p_near = near(after(p_near, two))
    for number in steps[:dp_steps][::-1]:
        one = summing.double(one, number)
        two = summing.double(two, number, p_near if number == 0 else None)
    mine = (one, two)
    other = tuple(summing.exchange(rows) for rows in mine)
    input_grad = input_grad + p_partner.astype(F32) + p_far.astype(F32) + p_near.astype(F32)
    bias_rows = [(0,), (1,)] + [(n,) for n in range(8, 14)] + [tuple(range(14, 14 + hidden // width))]
    shapes = [(hidden, width), (width, hidden)] + [(width, width)] * 4
    shapes += [(1, len(rows) * width) for rows in bias_rows]
    wide_grads = call(
        functools.partial(widen_kernel, bias_rows),
        (core.reshape(1).astype(jnp.int32), *mine, *other),
        (),
        [struct(shape, F32) for shape in shapes],
        [pltpu.VMEM(shape, F32) for shape in shapes] + [pltpu.SemaphoreType.DMA((len(shapes),))],
        0,
        limit=20 << 20,
    )
    g_w_down, g_w_up, g_w_out, g_w_query, g_w_key, g_w_value = wide_grads[:6]
    g_b_value, g_b_query, g_b_out, g_gain_one, g_shift_one, g_b_down, g_gain_two, g_shift_two, g_b_up = (
        v.reshape(-1) for v in wide_grads[6:]
    )
    return (
        layer, input_grad, g_w_query, g_b_query, g_w_key, g_w_value, g_b_value, g_w_out, g_b_out,
        g_gain_one, g_shift_one, g_w_up, g_b_up, g_w_down, g_b_down, g_gain_two, g_shift_two,
    )


def solution(mesh):
    rows = P(("dp", "seq"), None)
    return jax.shard_map(
        shards,
        mesh=mesh,
        in_specs=(rows, P("dp", None)) + (P(),) * 15 + (rows,),
        out_specs=(rows, rows) + (P(),) * 15,
        check_vma=False,
    )
```

profile of v0, /device:TPU:0, one launch (start us, length us, event | category | flops | bytes accessed | tf_op | source)
XLA Modules:
  0.0 220.0 jit_solution(397475036109793881)
XLA Ops:
  1.9 5.8 %collective-permute-start.3 = (bf16[1024,512]{1,0:T(8,128)(2,1)}, bf16[1024,512]{1,0:T(8,128)(2,1)S(1)}, u32[]{:S(2)}, u32[]{:S(2)}) collective-permute-start(bf16[1024,512]{1,0:T(8,128)(2,1)} %refs_15_.1), channel_id=1, source_target_pairs={{0,2},{2,4},{4,6},{3,1},{5,3},{7,5},{8,10},{10,12},{12,14},{11,9},... | collective-permute-start | bytes 3145736 | tf_op jit(solution)/shard_map/ppermute | solution.py:725
  8.7 17.4 %shard_map.305 = (s32[13]{0:T(128)}, bf16[1024,512]{1,0:T(8,128)(2,1)}, bf16[512,1024]{1,0:T(8,128)(2,1)}, bf16[2304,512]{1,0:T(8,128)(2,1)}, bf16[2304,512]{1,0...) custom-call(s32[1,8]{1,0:T(1,128)} %counts_ref.1, ...), custom_call_target="tpu_custom_call" | custom-call | flops 6979321856 | bytes 12922968 | tf_op jit(solution)/shard_map/pallas_call | solution.py:609
  26.1 8.6 %collective-permute-start.2 = (bf16[1024,512]{1,0:T(8,128)(2,1)S(1)}, bf16[1024,512]{1,0:T(8,128)(2,1)S(1)}, u32[]{:S(2)}, u32[]{:S(2)}) collective-permute-start(bf16[1024,512]{1,0:T(8,128)(2,1)S(1)} %collective-permute-done.1.refs_8_), channel_id=1, source_target_pairs={{0,1},{1,0},{2,3},{3,2},{4,5},{5,4},{6,7},{7,6},{8,9},{9,8},{10,11... | collective-permute-start | bytes 3145736 | tf_op jit(solution)/shard_map/ppermute | solution.py:717
  34.8 2.3 %collective-permute-done.2.xw_ref = bf16[1024,512]{1,0:T(8,128)(2,1)S(1)} collective-permute-done((bf16[1024,512]{1,0:T(8,128)(2,1)S(1)}, bf16[1024,512]{1,0:T(8,128)(2,1)S(1)}, u32[]{:S(2)}, u32[]{:S(2)}) %collective-permute-start.2) | collective-permute-done | bytes 1048608 | tf_op jit(solution)/shard_map/ppermute | solution.py:717
  38.0 46.6 %shard_map.306 = (bf16[1024,512]{1,0:T(8,128)(2,1)}, f32[1024,512]{1,0:T(8,128)}, bf16[1024,512]{1,0:T(8,128)(2,1)}, bf16[1024,512]{1,0:T(8,128)(2,1)}, bf16[102...) custom-call(s32[13]{0:T(128)} %get-tuple-element.60.meta_ref, ...), custom_call_target="tpu_custom_call" | custom-call | flops 32212254720 | bytes 31418420 | tf_op jit(solution)/shard_map/pallas_call | solution.py:609
  84.6 14.4 %collective-permute-start.4 = (bf16[2112,512]{1,0:T(8,128)(2,1)}, bf16[2112,512]{1,0:T(8,128)(2,1)S(1)}, u32[]{:S(2)}, u32[]{:S(2)}) collective-permute-start(bf16[2112,512]{1,0:T(8,128)(2,1)} %get-tuple-element.76), channel_id=1, source_target_pairs={{0,1},{1,0},{2,3},{3,2},{4,5},{5,4},{6,7},{7,6},{8,9},{9,8},{10,11... | collective-permute-start | bytes 6488072 | tf_op jit(solution)/shard_map/ppermute | solution.py:644
  99.1 5.5 %collective-permute-done.4 = bf16[2112,512]{1,0:T(8,128)(2,1)S(1)} collective-permute-done((bf16[2112,512]{1,0:T(8,128)(2,1)}, bf16[2112,512]{1,0:T(8,128)(2,1)S(1)}, u32[]{:S(2)}, u32[]{:S(2)}) %collective-permute-start.4) | collective-permute-done | bytes 2162720 | tf_op jit(solution)/shard_map/ppermute | solution.py:644
  105.9 2.9 %add.107 = bf16[2112,512]{1,0:T(8,128)(2,1)S(1)} add(bf16[2112,512]{1,0:T(8,128)(2,1)} %get-tuple-element.75, bf16[2112,512]{1,0:T(8,128)(2,1)} %copy-done.1) | non-fusion elementwise | flops 1081344 | bytes 6488064 | tf_op jit(solution)/shard_map/add | solution.py:807
  110.0 4.4 %collective-permute-start.8 = (bf16[544,512]{1,0:T(8,128)(2,1)}, bf16[544,512]{1,0:T(8,128)(2,1)}, u32[]{:S(2)}, u32[]{:S(2)}) collective-permute-start(bf16[544,512]{1,0:T(8,128)(2,1)} %get-tuple-element.107), channel_id=1, source_target_pairs={{0,8},{1,17},{2,10},{3,19},{4,12},{5,21},{6,14},{7,23},{8,0},{9,25... | collective-permute-start | bytes 1671176 | tf_op jit(solution)/shard_map/ppermute | solution.py:644
  114.4 2.5 %add.110 = bf16[1024,512]{1,0:T(8,128)(2,1)} add(bf16[1024,512]{1,0:T(8,128)(2,1)S(1)} %copy-done.4, bf16[1024,512]{1,0:T(8,128)(2,1)} %collective-permute-done.7) | non-fusion elementwise | flops 524288 | bytes 3145728 | tf_op jit(solution)/shard_map/add | solution.py:810
  117.1 5.1 %collective-permute-done.8 = bf16[544,512]{1,0:T(8,128)(2,1)} collective-permute-done((bf16[544,512]{1,0:T(8,128)(2,1)}, bf16[544,512]{1,0:T(8,128)(2,1)}, u32[]{:S(2)}, u32[]{:S(2)}) %collective-permute-start.8) | collective-permute-done | bytes 557088 | tf_op jit(solution)/shard_map/ppermute | solution.py:644
  128.3 5.3 %collective-permute-done.9 = bf16[512,512]{1,0:T(8,128)(2,1)S(1)} collective-permute-done((bf16[512,512]{1,0:T(8,128)(2,1)}, bf16[512,512]{1,0:T(8,128)(2,1)S(1)}, u32[]{:S(2)}, u32[]{:S(2)}) %collective-permute-start.9) | collective-permute-done | bytes 524320 | tf_op jit(solution)/shard_map/ppermute | solution.py:644
  136.3 26.6 %collective-permute-start.16 = (bf16[136,512]{1,0:T(8,128)(2,1)S(1)}, bf16[136,512]{1,0:T(8,128)(2,1)}, u32[]{:S(2)}, u32[]{:S(2)}) collective-permute-start(bf16[136,512]{1,0:T(8,128)(2,1)S(1)} %get-tuple-element.111), channel_id=1, source_target_pairs={{0,2},{1,3},{2,0},{3,1},{4,6},{5,7},{6,4},{7,5},{8,10},{9,11},{10,... | collective-permute-start | bytes 417800 | tf_op jit(solution)/shard_map/ppermute | solution.py:644
  163.9 3.4 %collective-permute-start.11 = (bf16[128,512]{1,0:T(8,128)(2,1)S(1)}, bf16[128,512]{1,0:T(8,128)(2,1)S(1)}, u32[]{:S(2)}, u32[]{:S(2)}) collective-permute-start(bf16[128,512]{1,0:T(8,128)(2,1)S(1)} %constant_dynamic-slice_fusion.4), channel_id=1, source_target_pairs={{0,2},{1,3},{2,0},{3,1},{4,6},{5,7},{6,4},{7,5},{8,10},{9,11},{10,... | collective-permute-start | bytes 393224 | tf_op jit(solution)/shard_map/ppermute | solution.py:644
  168.3 8.4 %collective-permute-start.17 = (bf16[136,512]{1,0:T(8,128)(2,1)S(1)}, bf16[136,512]{1,0:T(8,128)(2,1)S(1)}, u32[]{:S(2)}, u32[]{:S(2)}) collective-permute-start(bf16[136,512]{1,0:T(8,128)(2,1)S(1)} %add.135), channel_id=1, source_target_pairs={{0,4},{1,5},{2,6},{3,7},{4,0},{5,1},{6,2},{7,3},{8,12},{9,13},{10,... | collective-permute-start | bytes 417800 | tf_op jit(solution)/shard_map/ppermute | solution.py:644
  176.7 4.0 %collective-permute-start.12 = (bf16[128,512]{1,0:T(8,128)(2,1)S(1)}, bf16[128,512]{1,0:T(8,128)(2,1)S(1)}, u32[]{:S(2)}, u32[]{:S(2)}) collective-permute-start(bf16[128,512]{1,0:T(8,128)(2,1)S(1)} %dynamic-slice_add_fusion.2), channel_id=1, source_target_pairs={{0,4},{1,5},{2,6},{3,7},{4,0},{5,1},{6,2},{7,3},{8,12},{9,13},{10,... | collective-permute-start | bytes 393224 | tf_op jit(solution)/shard_map/ppermute | solution.py:644
  180.7 4.0 %collective-permute-done.17 = bf16[136,512]{1,0:T(8,128)(2,1)S(1)} collective-permute-done((bf16[136,512]{1,0:T(8,128)(2,1)S(1)}, bf16[136,512]{1,0:T(8,128)(2,1)S(1)}, u32[]{:S(2)}, u32[]{:S(2)}) %collective-permute-start.17) | collective-permute-done | bytes 139296 | tf_op jit(solution)/shard_map/ppermute | solution.py:644
  187.0 4.0 %collective-permute-done.18 = bf16[136,512]{1,0:T(8,128)(2,1)S(1)} collective-permute-done((bf16[136,512]{1,0:T(8,128)(2,1)S(1)}, bf16[136,512]{1,0:T(8,128)(2,1)S(1)}, u32[]{:S(2)}, u32[]{:S(2)}) %collective-permute-start.18) | collective-permute-done | bytes 139296 | tf_op jit(solution)/shard_map/ppermute | solution.py:644
  194.0 3.6 %collective-permute-done.19 = bf16[272,512]{1,0:T(8,128)(2,1)S(1)} collective-permute-done((bf16[272,512]{1,0:T(8,128)(2,1)S(1)}, bf16[272,512]{1,0:T(8,128)(2,1)S(1)}, u32[]{:S(2)}, u32[]{:S(2)}) %collective-permute-start.19) | collective-permute-done | bytes 278560 | tf_op jit(solution)/shard_map/ppermute | solution.py:644
  197.8 5.1 %collective-permute-done.21 = bf16[256,512]{1,0:T(8,128)(2,1)S(1)} collective-permute-done((bf16[256,512]{1,0:T(8,128)(2,1)S(1)}, bf16[256,512]{1,0:T(8,128)(2,1)S(1)}, u32[]{:S(2)}, u32[]{:S(2)}) %collective-permute-start.21) | collective-permute-done | bytes 262176 | tf_op jit(solution)/shard_map/ppermute | solution.py:644
  203.2 4.1 %collective-permute-done.20 = bf16[544,512]{1,0:T(8,128)(2,1)S(1)} collective-permute-done((bf16[544,512]{1,0:T(8,128)(2,1)S(1)}, bf16[544,512]{1,0:T(8,128)(2,1)S(1)}, u32[]{:S(2)}, u32[]{:S(2)}) %collective-permute-start.20) | collective-permute-done | bytes 557088 | tf_op jit(solution)/shard_map/ppermute | solution.py:644
  207.5 5.4 %collective-permute-done.22 = bf16[512,512]{1,0:T(8,128)(2,1)S(1)} collective-permute-done((bf16[512,512]{1,0:T(8,128)(2,1)S(1)}, bf16[512,512]{1,0:T(8,128)(2,1)S(1)}, u32[]{:S(2)}, u32[]{:S(2)}) %collective-permute-start.22) | collective-permute-done | bytes 524320 | tf_op jit(solution)/shard_map/ppermute | solution.py:644
  213.0 3.2 %convert_add_fusion = f32[1024,512]{1,0:T(8,128)} fusion(bf16[1024,512]{1,0:T(8,128)(2,1)S(1)} %collective-permute-done.14, bf16[1024,512]{1,0:T(8,128)(2,1)} %collective-permute-done.6, f32[1024,512]{1,0:T(8,128)S(1)} %copy-done.2, bf16[1024,512]{1,0:T(8,128)(2,1)S(1)} %collective-permute-done.5), kind=kLoop, calls=%fused_computation | loop fusion | flops 3145728 | bytes 7340032 | tf_op jit(solution)/shard_map/add | solution.py:832
  216.2 3.6 %shard_map.307 = (f32[1024,512]{1,0:T(8,128)}, f32[512,1024]{1,0:T(8,128)}, f32[512,512]{1,0:T(8,128)}, f32[512,512]{1,0:T(8,128)}, f32[512,512]{1,0:T(8,128)}, ...) custom-call(s32[1]{0:T(128)} %bitcast.10.core_ref, ...), custom_call_target="tpu_custom_call" | custom-call | bytes 12734468 | tf_op jit(solution)/shard_map/pallas_call | solution.py:609
  (82 shorter events, 22.5 us)
Async XLA Ops:
  0.7 7.0 %collective-permute-start = (bf16[1024,512]{1,0:T(8,128)(2,1)}, bf16[1024,512]{1,0:T(8,128)(2,1)S(1)}, u32[]{:S(2)}, u32[]{:S(2)}) collective-permute-start(bf16[1024,512]{1,0:T(8,128)(2,1)} %refs_15_.1), channel_id=1, source_target_pairs={{0,1},{1,0},{2,3},{3,2},{4,5},{5,4},{6,7},{7,6},{8,9},{9,8},{10,11... | collective-permute-start | bytes 3145736 | tf_op jit(solution)/shard_map/ppermute | solution.py:717
  1.2 24.9 %collective-permute-start.1 = (bf16[1024,512]{1,0:T(8,128)(2,1)}, bf16[1024,512]{1,0:T(8,128)(2,1)S(1)}, u32[]{:S(2)}, u32[]{:S(2)}) collective-permute-start(bf16[1024,512]{1,0:T(8,128)(2,1)} %refs_15_.1), channel_id=1, source_target_pairs={{1,2},{3,4},{5,6},{2,1},{4,3},{6,5},{9,10},{11,12},{13,14},{10,9},... | collective-permute-start | bytes 3145736 | tf_op jit(solution)/shard_map/ppermute | solution.py:721
  1.9 32.9 %collective-permute-start.3 = (bf16[1024,512]{1,0:T(8,128)(2,1)}, bf16[1024,512]{1,0:T(8,128)(2,1)S(1)}, u32[]{:S(2)}, u32[]{:S(2)}) collective-permute-start(bf16[1024,512]{1,0:T(8,128)(2,1)} %refs_15_.1), channel_id=1, source_target_pairs={{0,2},{2,4},{4,6},{3,1},{5,3},{7,5},{8,10},{10,12},{12,14},{11,9},... | collective-permute-start | bytes 3145736 | tf_op jit(solution)/shard_map/ppermute | solution.py:725
  26.1 10.9 %collective-permute-start.2 = (bf16[1024,512]{1,0:T(8,128)(2,1)S(1)}, bf16[1024,512]{1,0:T(8,128)(2,1)S(1)}, u32[]{:S(2)}, u32[]{:S(2)}) collective-permute-start(bf16[1024,512]{1,0:T(8,128)(2,1)S(1)} %collective-permute-done.1.refs_8_), channel_id=1, source_target_pairs={{0,1},{1,0},{2,3},{3,2},{4,5},{5,4},{6,7},{7,6},{8,9},{9,8},{10,11... | collective-permute-start | bytes 3145736 | tf_op jit(solution)/shard_map/ppermute | solution.py:717
  84.6 20.0 %collective-permute-start.4 = (bf16[2112,512]{1,0:T(8,128)(2,1)}, bf16[2112,512]{1,0:T(8,128)(2,1)S(1)}, u32[]{:S(2)}, u32[]{:S(2)}) collective-permute-start(bf16[2112,512]{1,0:T(8,128)(2,1)} %get-tuple-element.76), channel_id=1, source_target_pairs={{0,1},{1,0},{2,3},{3,2},{4,5},{5,4},{6,7},{7,6},{8,9},{9,8},{10,11... | collective-permute-start | bytes 6488072 | tf_op jit(solution)/shard_map/ppermute | solution.py:644
  99.0 15.4 %collective-permute-start.7 = (bf16[1024,512]{1,0:T(8,128)(2,1)}, bf16[1024,512]{1,0:T(8,128)(2,1)}, u32[]{:S(2)}, u32[]{:S(2)}) collective-permute-start(bf16[1024,512]{1,0:T(8,128)(2,1)} %get-tuple-element.81), channel_id=1, source_target_pairs={{0,1},{1,0},{2,3},{3,2},{4,5},{5,4},{6,7},{7,6},{8,9},{9,8},{10,11... | collective-permute-start | bytes 3145736 | tf_op jit(solution)/shard_map/ppermute | solution.py:717
  110.0 12.3 %collective-permute-start.8 = (bf16[544,512]{1,0:T(8,128)(2,1)}, bf16[544,512]{1,0:T(8,128)(2,1)}, u32[]{:S(2)}, u32[]{:S(2)}) collective-permute-start(bf16[544,512]{1,0:T(8,128)(2,1)} %get-tuple-element.107), channel_id=1, source_target_pairs={{0,8},{1,17},{2,10},{3,19},{4,12},{5,21},{6,14},{7,23},{8,0},{9,25... | collective-permute-start | bytes 1671176 | tf_op jit(solution)/shard_map/ppermute | solution.py:644
  117.0 17.0 %collective-permute-start.5 = (bf16[1024,512]{1,0:T(8,128)(2,1)}, bf16[1024,512]{1,0:T(8,128)(2,1)S(1)}, u32[]{:S(2)}, u32[]{:S(2)}) collective-permute-start(bf16[1024,512]{1,0:T(8,128)(2,1)} %get-tuple-element.77), channel_id=1, source_target_pairs={{0,1},{1,0},{2,3},{3,2},{4,5},{5,4},{6,7},{7,6},{8,9},{9,8},{10,11... | collective-permute-start | bytes 3145736 | tf_op jit(solution)/shard_map/ppermute | solution.py:717
  124.3 9.4 %collective-permute-start.9 = (bf16[512,512]{1,0:T(8,128)(2,1)}, bf16[512,512]{1,0:T(8,128)(2,1)S(1)}, u32[]{:S(2)}, u32[]{:S(2)}) collective-permute-start(bf16[512,512]{1,0:T(8,128)(2,1)} %constant_dynamic-slice_fusion.6), channel_id=1, source_target_pairs={{0,8},{1,17},{2,10},{3,19},{4,12},{5,21},{6,14},{7,23},{8,0},{9,25... | collective-permute-start | bytes 1572872 | tf_op jit(solution)/shard_map/ppermute | solution.py:644
  126.3 41.0 %collective-permute-start.6 = (bf16[1024,512]{1,0:T(8,128)(2,1)}, bf16[1024,512]{1,0:T(8,128)(2,1)}, u32[]{:S(2)}, u32[]{:S(2)}) collective-permute-start(bf16[1024,512]{1,0:T(8,128)(2,1)} %get-tuple-element.79), channel_id=1, source_target_pairs={{2,0},{4,2},{6,4},{1,3},{3,5},{5,7},{10,8},{12,10},{14,12},{9,11},... | collective-permute-start | bytes 3145736 | tf_op jit(solution)/shard_map/ppermute | solution.py:725
  128.3 6.9 %collective-permute-start.15 = (bf16[272,512]{1,0:T(8,128)(2,1)}, bf16[272,512]{1,0:T(8,128)(2,1)}, u32[]{:S(2)}, u32[]{:S(2)}) collective-permute-start(bf16[272,512]{1,0:T(8,128)(2,1)} %get-tuple-element.109), channel_id=1, source_target_pairs={{0,16},{1,9},{2,18},{3,11},{4,20},{5,13},{6,22},{7,15},{8,24},{9,1... | collective-permute-start | bytes 835592 | tf_op jit(solution)/shard_map/ppermute | solution.py:644
  133.8 29.1 %collective-permute-start.10 = (bf16[256,512]{1,0:T(8,128)(2,1)S(1)}, bf16[256,512]{1,0:T(8,128)(2,1)}, u32[]{:S(2)}, u32[]{:S(2)}) collective-permute-start(bf16[256,512]{1,0:T(8,128)(2,1)S(1)} %constant_dynamic-slice_fusion.5), channel_id=1, source_target_pairs={{0,16},{1,9},{2,18},{3,11},{4,20},{5,13},{6,22},{7,15},{8,24},{9,1... | collective-permute-start | bytes 786440 | tf_op jit(solution)/shard_map/ppermute | solution.py:644
  136.3 31.0 %collective-permute-start.16 = (bf16[136,512]{1,0:T(8,128)(2,1)S(1)}, bf16[136,512]{1,0:T(8,128)(2,1)}, u32[]{:S(2)}, u32[]{:S(2)}) collective-permute-start(bf16[136,512]{1,0:T(8,128)(2,1)S(1)} %get-tuple-element.111), channel_id=1, source_target_pairs={{0,2},{1,3},{2,0},{3,1},{4,6},{5,7},{6,4},{7,5},{8,10},{9,11},{10,... | collective-permute-start | bytes 417800 | tf_op jit(solution)/shard_map/ppermute | solution.py:644
  163.9 12.7 %collective-permute-start.11 = (bf16[128,512]{1,0:T(8,128)(2,1)S(1)}, bf16[128,512]{1,0:T(8,128)(2,1)S(1)}, u32[]{:S(2)}, u32[]{:S(2)}) collective-permute-start(bf16[128,512]{1,0:T(8,128)(2,1)S(1)} %constant_dynamic-slice_fusion.4), channel_id=1, source_target_pairs={{0,2},{1,3},{2,0},{3,1},{4,6},{5,7},{6,4},{7,5},{8,10},{9,11},{10,... | collective-permute-start | bytes 393224 | tf_op jit(solution)/shard_map/ppermute | solution.py:644
  168.3 16.4 %collective-permute-start.17 = (bf16[136,512]{1,0:T(8,128)(2,1)S(1)}, bf16[136,512]{1,0:T(8,128)(2,1)S(1)}, u32[]{:S(2)}, u32[]{:S(2)}) collective-permute-start(bf16[136,512]{1,0:T(8,128)(2,1)S(1)} %add.135), channel_id=1, source_target_pairs={{0,4},{1,5},{2,6},{3,7},{4,0},{5,1},{6,2},{7,3},{8,12},{9,13},{10,... | collective-permute-start | bytes 417800 | tf_op jit(solution)/shard_map/ppermute | solution.py:644
  176.7 9.7 %collective-permute-start.12 = (bf16[128,512]{1,0:T(8,128)(2,1)S(1)}, bf16[128,512]{1,0:T(8,128)(2,1)S(1)}, u32[]{:S(2)}, u32[]{:S(2)}) collective-permute-start(bf16[128,512]{1,0:T(8,128)(2,1)S(1)} %dynamic-slice_add_fusion.2), channel_id=1, source_target_pairs={{0,4},{1,5},{2,6},{3,7},{4,0},{5,1},{6,2},{7,3},{8,12},{9,13},{10,... | collective-permute-start | bytes 393224 | tf_op jit(solution)/shard_map/ppermute | solution.py:644
  184.8 6.2 %collective-permute-start.18 = (bf16[136,512]{1,0:T(8,128)(2,1)S(1)}, bf16[136,512]{1,0:T(8,128)(2,1)S(1)}, u32[]{:S(2)}, u32[]{:S(2)}) collective-permute-start(bf16[136,512]{1,0:T(8,128)(2,1)S(1)} %get-tuple-element.104), channel_id=1, source_target_pairs={{0,2},{1,3},{2,0},{3,1},{4,6},{5,7},{6,4},{7,5},{8,10},{9,11},{10,... | collective-permute-start | bytes 417800 | tf_op jit(solution)/shard_map/ppermute | solution.py:644
  186.5 5.9 %collective-permute-start.13 = (bf16[128,512]{1,0:T(8,128)(2,1)S(1)}, bf16[128,512]{1,0:T(8,128)(2,1)S(1)}, u32[]{:S(2)}, u32[]{:S(2)}) collective-permute-start(bf16[128,512]{1,0:T(8,128)(2,1)S(1)} %get-tuple-element.106), channel_id=1, source_target_pairs={{0,2},{1,3},{2,0},{3,1},{4,6},{5,7},{6,4},{7,5},{8,10},{9,11},{10,... | collective-permute-start | bytes 393224 | tf_op jit(solution)/shard_map/ppermute | solution.py:644
  191.0 6.6 %collective-permute-start.19 = (bf16[272,512]{1,0:T(8,128)(2,1)S(1)}, bf16[272,512]{1,0:T(8,128)(2,1)S(1)}, u32[]{:S(2)}, u32[]{:S(2)}) collective-permute-start(bf16[272,512]{1,0:T(8,128)(2,1)S(1)} %constant_dynamic-update-slice_fusion.8), channel_id=1, source_target_pairs={{0,16},{1,9},{2,18},{3,11},{4,20},{5,13},{6,22},{7,15},{8,24},{9,1... | collective-permute-start | bytes 835592 | tf_op jit(solution)/shard_map/ppermute | solution.py:644
  192.4 14.9 %collective-permute-start.14 = (bf16[1024,512]{1,0:T(8,128)(2,1)S(1)}, bf16[1024,512]{1,0:T(8,128)(2,1)S(1)}, u32[]{:S(2)}, u32[]{:S(2)}) collective-permute-start(bf16[1024,512]{1,0:T(8,128)(2,1)S(1)} %copy-done.3), channel_id=1, source_target_pairs={{1,2},{3,4},{5,6},{2,1},{4,3},{6,5},{9,10},{11,12},{13,14},{10,9},... | collective-permute-start | bytes 3145736 | tf_op jit(solution)/shard_map/ppermute | solution.py:721
  193.3 9.7 %collective-permute-start.21 = (bf16[256,512]{1,0:T(8,128)(2,1)S(1)}, bf16[256,512]{1,0:T(8,128)(2,1)S(1)}, u32[]{:S(2)}, u32[]{:S(2)}) collective-permute-start(bf16[256,512]{1,0:T(8,128)(2,1)S(1)} %constant_dynamic-update-slice_fusion.10), channel_id=1, source_target_pairs={{0,16},{1,9},{2,18},{3,11},{4,20},{5,13},{6,22},{7,15},{8,24},{9,1... | collective-permute-start | bytes 786440 | tf_op jit(solution)/shard_map/ppermute | solution.py:644
  197.7 9.6 %collective-permute-start.20 = (bf16[544,512]{1,0:T(8,128)(2,1)S(1)}, bf16[544,512]{1,0:T(8,128)(2,1)S(1)}, u32[]{:S(2)}, u32[]{:S(2)}) collective-permute-start(bf16[544,512]{1,0:T(8,128)(2,1)S(1)} %constant_dynamic-update-slice_fusion.6), channel_id=1, source_target_pairs={{0,8},{1,17},{2,10},{3,19},{4,12},{5,21},{6,14},{7,23},{8,0},{9,25... | collective-permute-start | bytes 1671176 | tf_op jit(solution)/shard_map/ppermute | solution.py:644
  203.0 9.9 %collective-permute-start.22 = (bf16[512,512]{1,0:T(8,128)(2,1)S(1)}, bf16[512,512]{1,0:T(8,128)(2,1)S(1)}, u32[]{:S(2)}, u32[]{:S(2)}) collective-permute-start(bf16[512,512]{1,0:T(8,128)(2,1)S(1)} %constant_dynamic-update-slice_fusion.2), channel_id=1, source_target_pairs={{0,8},{1,17},{2,10},{3,19},{4,12},{5,21},{6,14},{7,23},{8,0},{9,25... | collective-permute-start | bytes 1572872 | tf_op jit(solution)/shard_map/ppermute | solution.py:644
  207.3 8.9 %collective-permute-start.23 = (bf16[1088,512]{1,0:T(8,128)(2,1)S(1)}, bf16[1088,512]{1,0:T(8,128)(2,1)S(1)}, u32[]{:S(2)}, u32[]{:S(2)}) collective-permute-start(bf16[1088,512]{1,0:T(8,128)(2,1)S(1)} %constant_dynamic-update-slice_fusion.4.mine_one), channel_id=1, source_target_pairs={{0,1},{1,0},{2,3},{3,2},{4,5},{5,4},{6,7},{7,6},{8,9},{9,8},{10,11... | collective-permute-start | bytes 3342344 | tf_op jit(solution)/shard_map/ppermute | solution.py:644
  (10 other events, 99.2 us)
where the time goes:
time: 222 us; the launch traced here: 220 us
  starting transfers between devices  82.7 us (37%)
  Pallas kernels  67.6 us (30%)
  waiting for transfers between devices  48.6 us (22%)
  other arithmetic  13 us (6%)
  local copies, waits for them, and re-layouts  6.76 us (3%)
    pallas_call x3, Pallas kernels, call(): pl.pallas_call(kernel, out_shape=outputs, in_specs=smem * scalars + vmem(...  67.6 us
    ppermute x17, starting transfers between devices, exchange(): return lax.ppermute(rows, ('dp', 'seq'), pairs)  65 us
    ppermute x17, waiting for transfers between devices, exchange(): return lax.ppermute(rows, ('dp', 'seq'), pairs)  46.3 us
    ppermute x4, starting transfers between devices, swap(): return lax.ppermute(rows, 'seq', [(i, i ^ 1) for i in range(seq)])  9.27 us
    ppermute x2, starting transfers between devices, far(): lax.ppermute(rows, 'seq', [(b, a) for a, b in pairs] if back else pairs)  7.05 us
  transfers between devices with their start and end apart: 25, of which 13 were waited for; matrix products, arithmetic and copies ran while one was open for 7% of the time, Pallas kernels for 8%

commit v1 on v0

--- a/solution.py
+++ b/solution.py
@@ -813,7 +813,7 @@
     one, two = grads[:lead], grads[lead:]
     dp_steps = summing.dp_steps
     steps = list(range(len(summing.order) - 1))
-    others = {0: p_near, 1: p_partner, dp_steps: p_far}
+    others = {0: p_near, dp_steps: p_far, dp_steps + 1: p_partner}
     for number in steps:
         one = summing.halve(one, number, others.get(number))
         if number == 0:

time: 222 us -> 215 us (0.968); the launches traced: 220 us -> 216 us
  starting transfers between devices: 82.7 us -> 62.6 us
  Pallas kernels: 67.6 us -> 81 us
  waiting for transfers between devices: 48.6 us -> 56.5 us
  other arithmetic: 13 us -> 10.2 us
  local copies, waits for them, and re-layouts: 6.76 us -> 4.24 us
    ppermute x17, starting transfers between devices: 65 us -> 36.2 us  [exchange(): return lax.ppermute(rows, ('dp', 'seq'), pairs)]
    pallas_call x3, Pallas kernels: 67.6 us -> 81 us  [call(): pl.pallas_call(kernel, out_shape=outputs, in_specs=smem * scalars + vmem(...]
    ppermute x4, starting transfers between devices: 9.27 us -> 17.8 us  [swap(): return lax.ppermute(rows, 'seq', [(i, i ^ 1) for i in range(seq)])]
    ppermute x17, waiting for transfers between devices: 46.3 us -> 54.2 us  [exchange(): return lax.ppermute(rows, ('dp', 'seq'), pairs)]
    add x6, other arithmetic: 4.36 us -> 1.57 us  [halve(): return (mine if other is None else after(mine, other)) + got]
  transfers between devices with their start and end apart: 25 -> 25, of which waited for: 13 -> 14; matrix products, arithmetic and copies ran while one was open for 7% -> 5% of each run, Pallas kernels for 8% -> 10%
where the time goes in v1:
time: 215 us; the launch traced here: 216 us
  Pallas kernels  81 us (38%)
  starting transfers between devices  62.6 us (29%)
  waiting for transfers between devices  56.5 us (26%)
  other arithmetic  10.2 us (5%)
  local copies, waits for them, and re-layouts  4.24 us (2%)
    pallas_call x3, Pallas kernels, call(): pl.pallas_call(kernel, out_shape=outputs, in_specs=smem * scalars + vmem(...  81 us
    ppermute x17, waiting for transfers between devices, exchange(): return lax.ppermute(rows, ('dp', 'seq'), pairs)  54.2 us
    ppermute x17, starting transfers between devices, exchange(): return lax.ppermute(rows, ('dp', 'seq'), pairs)  36.2 us
    ppermute x4, starting transfers between devices, swap(): return lax.ppermute(rows, 'seq', [(i, i ^ 1) for i in range(seq)])  17.8 us
    ppermute x2, starting transfers between devices, far(): lax.ppermute(rows, 'seq', [(b, a) for a, b in pairs] if back else pairs)  7.06 us
  transfers between devices with their start and end apart: 25, of which 14 were waited for; matrix products, arithmetic and copies ran while one was open for 5% of the time, Pallas kernels for 10%

profile of v1, /device:TPU:0, one launch (start us, length us, event | category | flops | bytes accessed | tf_op | source)
XLA Modules:
  0.0 215.9 jit_solution(15879226470019350432)
XLA Ops:
  1.9 5.8 %collective-permute-start.3 = (bf16[1024,512]{1,0:T(8,128)(2,1)}, bf16[1024,512]{1,0:T(8,128)(2,1)S(1)}, u32[]{:S(2)}, u32[]{:S(2)}) collective-permute-start(bf16[1024,512]{1,0:T(8,128)(2,1)} %refs_15_.1), channel_id=1, source_target_pairs={{0,2},{2,4},{4,6},{3,1},{5,3},{7,5},{8,10},{10,12},{12,14},{11,9},... | collective-permute-start | bytes 3145736 | tf_op jit(solution)/shard_map/ppermute | solution.py:725
  8.7 20.9 %shard_map.305 = (s32[13]{0:T(128)}, bf16[1024,512]{1,0:T(8,128)(2,1)}, bf16[512,1024]{1,0:T(8,128)(2,1)}, bf16[2304,512]{1,0:T(8,128)(2,1)}, bf16[2304,512]{1,0...) custom-call(s32[1,8]{1,0:T(1,128)} %counts_ref.1, ...), custom_call_target="tpu_custom_call" | custom-call | flops 6979321856 | bytes 12922968 | tf_op jit(solution)/shard_map/pallas_call | solution.py:609
  29.6 17.2 %collective-permute-start.2 = (bf16[1024,512]{1,0:T(8,128)(2,1)S(1)}, bf16[1024,512]{1,0:T(8,128)(2,1)S(1)}, u32[]{:S(2)}, u32[]{:S(2)}) collective-permute-start(bf16[1024,512]{1,0:T(8,128)(2,1)S(1)} %collective-permute-done.1.refs_8_), channel_id=1, source_target_pairs={{0,1},{1,0},{2,3},{3,2},{4,5},{5,4},{6,7},{7,6},{8,9},{9,8},{10,11... | collective-permute-start | bytes 3145736 | tf_op jit(solution)/shard_map/ppermute | solution.py:717
  46.8 2.3 %collective-permute-done.2.xw_ref = bf16[1024,512]{1,0:T(8,128)(2,1)S(1)} collective-permute-done((bf16[1024,512]{1,0:T(8,128)(2,1)S(1)}, bf16[1024,512]{1,0:T(8,128)(2,1)S(1)}, u32[]{:S(2)}, u32[]{:S(2)}) %collective-permute-start.2) | collective-permute-done | bytes 1048608 | tf_op jit(solution)/shard_map/ppermute | solution.py:717
  50.1 56.5 %shard_map.306 = (bf16[1024,512]{1,0:T(8,128)(2,1)}, f32[1024,512]{1,0:T(8,128)}, bf16[1024,512]{1,0:T(8,128)(2,1)}, bf16[1024,512]{1,0:T(8,128)(2,1)}, bf16[102...) custom-call(s32[13]{0:T(128)} %get-tuple-element.59.meta_ref, ...), custom_call_target="tpu_custom_call" | custom-call | flops 32212254720 | bytes 31418420 | tf_op jit(solution)/shard_map/pallas_call | solution.py:609
  106.6 18.0 %collective-permute-start.4 = (bf16[2112,512]{1,0:T(8,128)(2,1)}, bf16[2112,512]{1,0:T(8,128)(2,1)}, u32[]{:S(2)}, u32[]{:S(2)}) collective-permute-start(bf16[2112,512]{1,0:T(8,128)(2,1)} %get-tuple-element.75), channel_id=1, source_target_pairs={{0,1},{1,0},{2,3},{3,2},{4,5},{5,4},{6,7},{7,6},{8,9},{9,8},{10,11... | collective-permute-start | bytes 6488072 | tf_op jit(solution)/shard_map/ppermute | solution.py:644
  124.7 4.1 %collective-permute-done.4 = bf16[2112,512]{1,0:T(8,128)(2,1)} collective-permute-done((bf16[2112,512]{1,0:T(8,128)(2,1)}, bf16[2112,512]{1,0:T(8,128)(2,1)}, u32[]{:S(2)}, u32[]{:S(2)}) %collective-permute-start.4) | collective-permute-done | bytes 2162720 | tf_op jit(solution)/shard_map/ppermute | solution.py:644
  128.9 2.9 %add.107 = bf16[2112,512]{1,0:T(8,128)(2,1)S(1)} add(bf16[2112,512]{1,0:T(8,128)(2,1)} %get-tuple-element.74, bf16[2112,512]{1,0:T(8,128)(2,1)} %collective-permute-done.4) | non-fusion elementwise | flops 1081344 | bytes 6488064 | tf_op jit(solution)/shard_map/add | solution.py:807
  133.3 2.5 %add.110 = bf16[1024,512]{1,0:T(8,128)(2,1)} add(bf16[1024,512]{1,0:T(8,128)(2,1)S(1)} %copy-done.3, bf16[1024,512]{1,0:T(8,128)(2,1)} %collective-permute-done.7) | non-fusion elementwise | flops 524288 | bytes 3145728 | tf_op jit(solution)/shard_map/add | solution.py:810
  135.9 6.9 %collective-permute-done.8 = bf16[544,512]{1,0:T(8,128)(2,1)} collective-permute-done((bf16[544,512]{1,0:T(8,128)(2,1)}, bf16[544,512]{1,0:T(8,128)(2,1)}, u32[]{:S(2)}, u32[]{:S(2)}) %collective-permute-start.8) | collective-permute-done | bytes 557088 | tf_op jit(solution)/shard_map/ppermute | solution.py:644
  145.6 10.6 %collective-permute-done.9 = bf16[512,512]{1,0:T(8,128)(2,1)S(1)} collective-permute-done((bf16[512,512]{1,0:T(8,128)(2,1)S(1)}, bf16[512,512]{1,0:T(8,128)(2,1)S(1)}, u32[]{:S(2)}, u32[]{:S(2)}) %collective-permute-start.9) | collective-permute-done | bytes 524320 | tf_op jit(solution)/shard_map/ppermute | solution.py:644
  156.7 6.1 %collective-permute-done.10 = bf16[256,512]{1,0:T(8,128)(2,1)S(1)} collective-permute-done((bf16[256,512]{1,0:T(8,128)(2,1)S(1)}, bf16[256,512]{1,0:T(8,128)(2,1)S(1)}, u32[]{:S(2)}, u32[]{:S(2)}) %collective-permute-start.10) | collective-permute-done | bytes 262176 | tf_op jit(solution)/shard_map/ppermute | solution.py:644
  163.0 1.8 collective-permute-done.16
  164.8 11.7 %collective-permute-start.17 = (bf16[136,512]{1,0:T(8,128)(2,1)S(1)}, bf16[136,512]{1,0:T(8,128)(2,1)S(1)}, u32[]{:S(2)}, u32[]{:S(2)}) collective-permute-start(bf16[136,512]{1,0:T(8,128)(2,1)S(1)} %add.135), channel_id=1, source_target_pairs={{0,4},{1,5},{2,6},{3,7},{4,0},{5,1},{6,2},{7,3},{8,12},{9,13},{10,... | collective-permute-start | bytes 417800 | tf_op jit(solution)/shard_map/ppermute | solution.py:644
  176.6 2.8 %collective-permute-start.12 = (bf16[128,512]{1,0:T(8,128)(2,1)S(1)}, bf16[128,512]{1,0:T(8,128)(2,1)S(1)}, u32[]{:S(2)}, u32[]{:S(2)}) collective-permute-start(bf16[128,512]{1,0:T(8,128)(2,1)S(1)} %dynamic-slice_add_fusion.3), channel_id=1, source_target_pairs={{0,4},{1,5},{2,6},{3,7},{4,0},{5,1},{6,2},{7,3},{8,12},{9,13},{10,... | collective-permute-start | bytes 393224 | tf_op jit(solution)/shard_map/ppermute | solution.py:644
  180.6 1.8 collective-permute-start.18
  182.4 1.8 collective-permute-done.12
  185.8 3.5 %collective-permute-done.13 = bf16[128,512]{1,0:T(8,128)(2,1)S(1)} collective-permute-done((bf16[128,512]{1,0:T(8,128)(2,1)S(1)}, bf16[128,512]{1,0:T(8,128)(2,1)S(1)}, u32[]{:S(2)}, u32[]{:S(2)}) %collective-permute-start.13) | collective-permute-done | bytes 131104 | tf_op jit(solution)/shard_map/ppermute | solution.py:644
  190.3 2.1 collective-permute-done.19
  193.2 5.4 %collective-permute-done.21 = bf16[256,512]{1,0:T(8,128)(2,1)S(1)} collective-permute-done((bf16[256,512]{1,0:T(8,128)(2,1)S(1)}, bf16[256,512]{1,0:T(8,128)(2,1)S(1)}, u32[]{:S(2)}, u32[]{:S(2)}) %collective-permute-start.21) | collective-permute-done | bytes 262176 | tf_op jit(solution)/shard_map/ppermute | solution.py:644
  199.0 4.3 %collective-permute-done.20 = bf16[544,512]{1,0:T(8,128)(2,1)S(1)} collective-permute-done((bf16[544,512]{1,0:T(8,128)(2,1)S(1)}, bf16[544,512]{1,0:T(8,128)(2,1)S(1)}, u32[]{:S(2)}, u32[]{:S(2)}) %collective-permute-start.20) | collective-permute-done | bytes 557088 | tf_op jit(solution)/shard_map/ppermute | solution.py:644
  203.5 5.4 %collective-permute-done.22 = bf16[512,512]{1,0:T(8,128)(2,1)S(1)} collective-permute-done((bf16[512,512]{1,0:T(8,128)(2,1)S(1)}, bf16[512,512]{1,0:T(8,128)(2,1)S(1)}, u32[]{:S(2)}, u32[]{:S(2)}) %collective-permute-start.22) | collective-permute-done | bytes 524320 | tf_op jit(solution)/shard_map/ppermute | solution.py:644
  209.0 3.1 %convert_add_fusion = f32[1024,512]{1,0:T(8,128)} fusion(bf16[1024,512]{1,0:T(8,128)(2,1)S(1)} %collective-permute-done.14, bf16[1024,512]{1,0:T(8,128)(2,1)} %collective-permute-done.6, f32[1024,512]{1,0:T(8,128)S(1)} %copy-done.1, bf16[1024,512]{1,0:T(8,128)(2,1)S(1)} %collective-permute-done.5), kind=kLoop, calls=%fused_computation | loop fusion | flops 3145728 | bytes 7340032 | tf_op jit(solution)/shard_map/add | solution.py:832
  212.2 3.6 %shard_map.307 = (f32[1024,512]{1,0:T(8,128)}, f32[512,1024]{1,0:T(8,128)}, f32[512,512]{1,0:T(8,128)}, f32[512,512]{1,0:T(8,128)}, f32[512,512]{1,0:T(8,128)}, ...) custom-call(s32[1]{0:T(128)} %bitcast.10.core_ref, ...), custom_call_target="tpu_custom_call" | custom-call | bytes 12734468 | tf_op jit(solution)/shard_map/pallas_call | solution.py:609
  (82 shorter events, 13.3 us)
Async XLA Ops:
  0.7 7.0 %collective-permute-start = (bf16[1024,512]{1,0:T(8,128)(2,1)}, bf16[1024,512]{1,0:T(8,128)(2,1)S(1)}, u32[]{:S(2)}, u32[]{:S(2)}) collective-permute-start(bf16[1024,512]{1,0:T(8,128)(2,1)} %refs_15_.1), channel_id=1, source_target_pairs={{0,1},{1,0},{2,3},{3,2},{4,5},{5,4},{6,7},{7,6},{8,9},{9,8},{10,11... | collective-permute-start | bytes 3145736 | tf_op jit(solution)/shard_map/ppermute | solution.py:717
  1.2 28.4 %collective-permute-start.1 = (bf16[1024,512]{1,0:T(8,128)(2,1)}, bf16[1024,512]{1,0:T(8,128)(2,1)S(1)}, u32[]{:S(2)}, u32[]{:S(2)}) collective-permute-start(bf16[1024,512]{1,0:T(8,128)(2,1)} %refs_15_.1), channel_id=1, source_target_pairs={{1,2},{3,4},{5,6},{2,1},{4,3},{6,5},{9,10},{11,12},{13,14},{10,9},... | collective-permute-start | bytes 3145736 | tf_op jit(solution)/shard_map/ppermute | solution.py:721
  1.9 44.9 %collective-permute-start.3 = (bf16[1024,512]{1,0:T(8,128)(2,1)}, bf16[1024,512]{1,0:T(8,128)(2,1)S(1)}, u32[]{:S(2)}, u32[]{:S(2)}) collective-permute-start(bf16[1024,512]{1,0:T(8,128)(2,1)} %refs_15_.1), channel_id=1, source_target_pairs={{0,2},{2,4},{4,6},{3,1},{5,3},{7,5},{8,10},{10,12},{12,14},{11,9},... | collective-permute-start | bytes 3145736 | tf_op jit(solution)/shard_map/ppermute | solution.py:725
  29.6 19.5 %collective-permute-start.2 = (bf16[1024,512]{1,0:T(8,128)(2,1)S(1)}, bf16[1024,512]{1,0:T(8,128)(2,1)S(1)}, u32[]{:S(2)}, u32[]{:S(2)}) collective-permute-start(bf16[1024,512]{1,0:T(8,128)(2,1)S(1)} %collective-permute-done.1.refs_8_), channel_id=1, source_target_pairs={{0,1},{1,0},{2,3},{3,2},{4,5},{5,4},{6,7},{7,6},{8,9},{9,8},{10,11... | collective-permute-start | bytes 3145736 | tf_op jit(solution)/shard_map/ppermute | solution.py:717
  106.6 22.3 %collective-permute-start.4 = (bf16[2112,512]{1,0:T(8,128)(2,1)}, bf16[2112,512]{1,0:T(8,128)(2,1)}, u32[]{:S(2)}, u32[]{:S(2)}) collective-permute-start(bf16[2112,512]{1,0:T(8,128)(2,1)} %get-tuple-element.75), channel_id=1, source_target_pairs={{0,1},{1,0},{2,3},{3,2},{4,5},{5,4},{6,7},{7,6},{8,9},{9,8},{10,11... | collective-permute-start | bytes 6488072 | tf_op jit(solution)/shard_map/ppermute | solution.py:644
  124.6 8.3 %collective-permute-start.7 = (bf16[1024,512]{1,0:T(8,128)(2,1)}, bf16[1024,512]{1,0:T(8,128)(2,1)}, u32[]{:S(2)}, u32[]{:S(2)}) collective-permute-start(bf16[1024,512]{1,0:T(8,128)(2,1)} %get-tuple-element.80), channel_id=1, source_target_pairs={{0,1},{1,0},{2,3},{3,2},{4,5},{5,4},{6,7},{7,6},{8,9},{9,8},{10,11... | collective-permute-start | bytes 3145736 | tf_op jit(solution)/shard_map/ppermute | solution.py:717
  132.9 9.8 %collective-permute-start.8 = (bf16[544,512]{1,0:T(8,128)(2,1)}, bf16[544,512]{1,0:T(8,128)(2,1)}, u32[]{:S(2)}, u32[]{:S(2)}) collective-permute-start(bf16[544,512]{1,0:T(8,128)(2,1)} %get-tuple-element.105), channel_id=1, source_target_pairs={{0,8},{1,17},{2,10},{3,19},{4,12},{5,21},{6,14},{7,23},{8,0},{9,25... | collective-permute-start | bytes 1671176 | tf_op jit(solution)/shard_map/ppermute | solution.py:644
  144.0 12.2 %collective-permute-start.9 = (bf16[512,512]{1,0:T(8,128)(2,1)S(1)}, bf16[512,512]{1,0:T(8,128)(2,1)S(1)}, u32[]{:S(2)}, u32[]{:S(2)}) collective-permute-start(bf16[512,512]{1,0:T(8,128)(2,1)S(1)} %constant_dynamic-slice_fusion.5), channel_id=1, source_target_pairs={{0,8},{1,17},{2,10},{3,19},{4,12},{5,21},{6,14},{7,23},{8,0},{9,25... | collective-permute-start | bytes 1572872 | tf_op jit(solution)/shard_map/ppermute | solution.py:644
  144.2 18.9 %collective-permute-start.6 = (bf16[1024,512]{1,0:T(8,128)(2,1)}, bf16[1024,512]{1,0:T(8,128)(2,1)}, u32[]{:S(2)}, u32[]{:S(2)}) collective-permute-start(bf16[1024,512]{1,0:T(8,128)(2,1)} %get-tuple-element.78), channel_id=1, source_target_pairs={{2,0},{4,2},{6,4},{1,3},{3,5},{5,7},{10,8},{12,10},{14,12},{9,11},... | collective-permute-start | bytes 3145736 | tf_op jit(solution)/shard_map/ppermute | solution.py:725
  145.5 11.0 %collective-permute-start.15 = (bf16[272,512]{1,0:T(8,128)(2,1)S(1)}, bf16[272,512]{1,0:T(8,128)(2,1)S(1)}, u32[]{:S(2)}, u32[]{:S(2)}) collective-permute-start(bf16[272,512]{1,0:T(8,128)(2,1)S(1)} %constant_dynamic-slice_fusion.2), channel_id=1, source_target_pairs={{0,16},{1,9},{2,18},{3,11},{4,20},{5,13},{6,22},{7,15},{8,24},{9,1... | collective-permute-start | bytes 835592 | tf_op jit(solution)/shard_map/ppermute | solution.py:644
  156.4 6.4 %collective-permute-start.10 = (bf16[256,512]{1,0:T(8,128)(2,1)S(1)}, bf16[256,512]{1,0:T(8,128)(2,1)S(1)}, u32[]{:S(2)}, u32[]{:S(2)}) collective-permute-start(bf16[256,512]{1,0:T(8,128)(2,1)S(1)} %constant_dynamic-slice_fusion.4), channel_id=1, source_target_pairs={{0,16},{1,9},{2,18},{3,11},{4,20},{5,13},{6,22},{7,15},{8,24},{9,1... | collective-permute-start | bytes 786440 | tf_op jit(solution)/shard_map/ppermute | solution.py:644
  156.6 8.2 %collective-permute-start.16 = (bf16[136,512]{1,0:T(8,128)(2,1)S(1)}, bf16[136,512]{1,0:T(8,128)(2,1)S(1)}, u32[]{:S(2)}, u32[]{:S(2)}) collective-permute-start(bf16[136,512]{1,0:T(8,128)(2,1)S(1)} %get-tuple-element.107), channel_id=1, source_target_pairs={{0,2},{1,3},{2,0},{3,1},{4,6},{5,7},{6,4},{7,5},{8,10},{9,11},{10,... | collective-permute-start | bytes 417800 | tf_op jit(solution)/shard_map/ppermute | solution.py:644
  162.9 13.6 %collective-permute-start.11 = (bf16[128,512]{1,0:T(8,128)(2,1)S(1)}, bf16[128,512]{1,0:T(8,128)(2,1)S(1)}, u32[]{:S(2)}, u32[]{:S(2)}) collective-permute-start(bf16[128,512]{1,0:T(8,128)(2,1)S(1)} %constant_dynamic-slice_fusion.3), channel_id=1, source_target_pairs={{0,2},{1,3},{2,0},{3,1},{4,6},{5,7},{6,4},{7,5},{8,10},{9,11},{10,... | collective-permute-start | bytes 393224 | tf_op jit(solution)/shard_map/ppermute | solution.py:644
  164.8 15.6 %collective-permute-start.17 = (bf16[136,512]{1,0:T(8,128)(2,1)S(1)}, bf16[136,512]{1,0:T(8,128)(2,1)S(1)}, u32[]{:S(2)}, u32[]{:S(2)}) collective-permute-start(bf16[136,512]{1,0:T(8,128)(2,1)S(1)} %add.135), channel_id=1, source_target_pairs={{0,4},{1,5},{2,6},{3,7},{4,0},{5,1},{6,2},{7,3},{8,12},{9,13},{10,... | collective-permute-start | bytes 417800 | tf_op jit(solution)/shard_map/ppermute | solution.py:644
  176.6 7.6 %collective-permute-start.12 = (bf16[128,512]{1,0:T(8,128)(2,1)S(1)}, bf16[128,512]{1,0:T(8,128)(2,1)S(1)}, u32[]{:S(2)}, u32[]{:S(2)}) collective-permute-start(bf16[128,512]{1,0:T(8,128)(2,1)S(1)} %dynamic-slice_add_fusion.3), channel_id=1, source_target_pairs={{0,4},{1,5},{2,6},{3,7},{4,0},{5,1},{6,2},{7,3},{8,12},{9,13},{10,... | collective-permute-start | bytes 393224 | tf_op jit(solution)/shard_map/ppermute | solution.py:644
  180.6 5.2 %collective-permute-start.18 = (bf16[136,512]{1,0:T(8,128)(2,1)S(1)}, bf16[136,512]{1,0:T(8,128)(2,1)S(1)}, u32[]{:S(2)}, u32[]{:S(2)}) collective-permute-start(bf16[136,512]{1,0:T(8,128)(2,1)S(1)} %get-tuple-element.102), channel_id=1, source_target_pairs={{0,2},{1,3},{2,0},{3,1},{4,6},{5,7},{6,4},{7,5},{8,10},{9,11},{10,... | collective-permute-start | bytes 417800 | tf_op jit(solution)/shard_map/ppermute | solution.py:644
  184.3 5.0 %collective-permute-start.13 = (bf16[128,512]{1,0:T(8,128)(2,1)S(1)}, bf16[128,512]{1,0:T(8,128)(2,1)S(1)}, u32[]{:S(2)}, u32[]{:S(2)}) collective-permute-start(bf16[128,512]{1,0:T(8,128)(2,1)S(1)} %get-tuple-element.104), channel_id=1, source_target_pairs={{0,2},{1,3},{2,0},{3,1},{4,6},{5,7},{6,4},{7,5},{8,10},{9,11},{10,... | collective-permute-start | bytes 393224 | tf_op jit(solution)/shard_map/ppermute | solution.py:644
  185.7 6.6 %collective-permute-start.19 = (bf16[272,512]{1,0:T(8,128)(2,1)S(1)}, bf16[272,512]{1,0:T(8,128)(2,1)S(1)}, u32[]{:S(2)}, u32[]{:S(2)}) collective-permute-start(bf16[272,512]{1,0:T(8,128)(2,1)S(1)} %constant_dynamic-update-slice_fusion.8), channel_id=1, source_target_pairs={{0,16},{1,9},{2,18},{3,11},{4,20},{5,13},{6,22},{7,15},{8,24},{9,1... | collective-permute-start | bytes 835592 | tf_op jit(solution)/shard_map/ppermute | solution.py:644
  189.4 14.0 %collective-permute-start.14 = (bf16[1024,512]{1,0:T(8,128)(2,1)S(1)}, bf16[1024,512]{1,0:T(8,128)(2,1)S(1)}, u32[]{:S(2)}, u32[]{:S(2)}) collective-permute-start(bf16[1024,512]{1,0:T(8,128)(2,1)S(1)} %copy-done.2), channel_id=1, source_target_pairs={{1,2},{3,4},{5,6},{2,1},{4,3},{6,5},{9,10},{11,12},{13,14},{10,9},... | collective-permute-start | bytes 3145736 | tf_op jit(solution)/shard_map/ppermute | solution.py:721
  190.2 8.5 %collective-permute-start.21 = (bf16[256,512]{1,0:T(8,128)(2,1)S(1)}, bf16[256,512]{1,0:T(8,128)(2,1)S(1)}, u32[]{:S(2)}, u32[]{:S(2)}) collective-permute-start(bf16[256,512]{1,0:T(8,128)(2,1)S(1)} %constant_dynamic-update-slice_fusion.10), channel_id=1, source_target_pairs={{0,16},{1,9},{2,18},{3,11},{4,20},{5,13},{6,22},{7,15},{8,24},{9,1... | collective-permute-start | bytes 786440 | tf_op jit(solution)/shard_map/ppermute | solution.py:644
  192.4 10.9 %collective-permute-start.20 = (bf16[544,512]{1,0:T(8,128)(2,1)S(1)}, bf16[544,512]{1,0:T(8,128)(2,1)S(1)}, u32[]{:S(2)}, u32[]{:S(2)}) collective-permute-start(bf16[544,512]{1,0:T(8,128)(2,1)S(1)} %constant_dynamic-update-slice_fusion.6), channel_id=1, source_target_pairs={{0,8},{1,17},{2,10},{3,19},{4,12},{5,21},{6,14},{7,23},{8,0},{9,25... | collective-permute-start | bytes 1671176 | tf_op jit(solution)/shard_map/ppermute | solution.py:644
  198.7 10.2 %collective-permute-start.22 = (bf16[512,512]{1,0:T(8,128)(2,1)S(1)}, bf16[512,512]{1,0:T(8,128)(2,1)S(1)}, u32[]{:S(2)}, u32[]{:S(2)}) collective-permute-start(bf16[512,512]{1,0:T(8,128)(2,1)S(1)} %constant_dynamic-update-slice_fusion.2), channel_id=1, source_target_pairs={{0,8},{1,17},{2,10},{3,19},{4,12},{5,21},{6,14},{7,23},{8,0},{9,25... | collective-permute-start | bytes 1572872 | tf_op jit(solution)/shard_map/ppermute | solution.py:644
  198.8 10.2 %collective-permute-start.5 = (bf16[1024,512]{1,0:T(8,128)(2,1)S(1)}, bf16[1024,512]{1,0:T(8,128)(2,1)S(1)}, u32[]{:S(2)}, u32[]{:S(2)}) collective-permute-start(bf16[1024,512]{1,0:T(8,128)(2,1)S(1)} %copy-done.4), channel_id=1, source_target_pairs={{0,1},{1,0},{2,3},{3,2},{4,5},{5,4},{6,7},{7,6},{8,9},{9,8},{10,11... | collective-permute-start | bytes 3145736 | tf_op jit(solution)/shard_map/ppermute | solution.py:717
  203.3 8.8 %collective-permute-start.23 = (bf16[1088,512]{1,0:T(8,128)(2,1)S(1)}, bf16[1088,512]{1,0:T(8,128)(2,1)S(1)}, u32[]{:S(2)}, u32[]{:S(2)}) collective-permute-start(bf16[1088,512]{1,0:T(8,128)(2,1)S(1)} %constant_dynamic-update-slice_fusion.4.mine_one), channel_id=1, source_target_pairs={{0,1},{1,0},{2,3},{3,2},{4,5},{5,4},{6,7},{7,6},{8,9},{9,8},{10,11... | collective-permute-start | bytes 3342344 | tf_op jit(solution)/shard_map/ppermute | solution.py:644
  (10 other events, 95.3 us)

commit v2 on v1

--- a/solution.py
+++ b/solution.py
@@ -813,7 +813,7 @@
     one, two = grads[:lead], grads[lead:]
     dp_steps = summing.dp_steps
     steps = list(range(len(summing.order) - 1))
-    others = {0: p_near, dp_steps: p_far, dp_steps + 1: p_partner}
+    others = {dp_steps: p_far}
     for number in steps:
         one = summing.halve(one, number, others.get(number))
         if number == 0:

time: 215 us -> 219 us (1.019)
  starting transfers between devices: 62.6 us -> 86.5 us
  Pallas kernels: 81 us -> 69.2 us
  waiting for transfers between devices: 56.5 us -> 49.5 us
    ppermute x17, starting transfers between devices: 36.2 us -> 66.3 us  [exchange(): return lax.ppermute(rows, ('dp', 'seq'), pairs)]
    pallas_call x3, Pallas kernels: 81 us -> 69.2 us  [call(): pl.pallas_call(kernel, out_shape=outputs, in_specs=smem * scalars + vmem(...]
    ppermute x17, waiting for transfers between devices: 54.2 us -> 47.2 us  [exchange(): return lax.ppermute(rows, ('dp', 'seq'), pairs)]
    ppermute x4, starting transfers between devices: 17.8 us -> 11.7 us  [swap(): return lax.ppermute(rows, 'seq', [(i, i ^ 1) for i in range(seq)])]
  transfers between devices with their start and end apart: 25 -> 25, of which waited for: 14 -> 14; matrix products, arithmetic and copies ran while one was open for 5% -> 3% of each run, Pallas kernels for 10% -> 8%
where the time goes in v2:
time: 219 us
  starting transfers between devices  86.5 us (39%)
  Pallas kernels  69.2 us (32%)
  waiting for transfers between devices  49.5 us (23%)
  other arithmetic  8.95 us (4%)
  local copies, waits for them, and re-layouts  3.65 us (2%)
    pallas_call x3, Pallas kernels, call(): pl.pallas_call(kernel, out_shape=outputs, in_specs=smem * scalars + vmem(...  69.2 us
    ppermute x17, starting transfers between devices, exchange(): return lax.ppermute(rows, ('dp', 'seq'), pairs)  66.3 us
    ppermute x17, waiting for transfers between devices, exchange(): return lax.ppermute(rows, ('dp', 'seq'), pairs)  47.2 us
    ppermute x4, starting transfers between devices, swap(): return lax.ppermute(rows, 'seq', [(i, i ^ 1) for i in range(seq)])  11.7 us
    ppermute x2, starting transfers between devices, far(): lax.ppermute(rows, 'seq', [(b, a) for a, b in pairs] if back else pairs)  7.06 us
  transfers between devices with their start and end apart: 25, of which 14 were waited for; matrix products, arithmetic and copies ran while one was open for 3% of the time, Pallas kernels for 8%

profile of v2, /device:TPU:0, one launch (start us, length us, event | category | flops | bytes accessed | tf_op | source)
XLA Modules:
  0.0 219.2 jit_solution(3624322055027428086)
XLA Ops:
  1.9 5.8 %collective-permute-start.3 = (bf16[1024,512]{1,0:T(8,128)(2,1)}, bf16[1024,512]{1,0:T(8,128)(2,1)S(1)}, u32[]{:S(2)}, u32[]{:S(2)}) collective-permute-start(bf16[1024,512]{1,0:T(8,128)(2,1)} %refs_15_.1), channel_id=1, source_target_pairs={{0,2},{2,4},{4,6},{3,1},{5,3},{7,5},{8,10},{10,12},{12,14},{11,9},... | collective-permute-start | bytes 3145736 | tf_op jit(solution)/shard_map/ppermute | solution.py:725
  8.7 17.9 %shard_map.305 = (s32[13]{0:T(128)}, bf16[1024,512]{1,0:T(8,128)(2,1)}, bf16[512,1024]{1,0:T(8,128)(2,1)}, bf16[2304,512]{1,0:T(8,128)(2,1)}, bf16[2304,512]{1,0...) custom-call(s32[1,8]{1,0:T(1,128)} %counts_ref.1, ...), custom_call_target="tpu_custom_call" | custom-call | flops 6979321856 | bytes 12922968 | tf_op jit(solution)/shard_map/pallas_call | solution.py:609
  26.5 11.1 %collective-permute-start.2 = (bf16[1024,512]{1,0:T(8,128)(2,1)S(1)}, bf16[1024,512]{1,0:T(8,128)(2,1)S(1)}, u32[]{:S(2)}, u32[]{:S(2)}) collective-permute-start(bf16[1024,512]{1,0:T(8,128)(2,1)S(1)} %collective-permute-done.1.refs_8_), channel_id=1, source_target_pairs={{0,1},{1,0},{2,3},{3,2},{4,5},{5,4},{6,7},{7,6},{8,9},{9,8},{10,11... | collective-permute-start | bytes 3145736 | tf_op jit(solution)/shard_map/ppermute | solution.py:717
  37.7 2.3 %collective-permute-done.2.xw_ref = bf16[1024,512]{1,0:T(8,128)(2,1)S(1)} collective-permute-done((bf16[1024,512]{1,0:T(8,128)(2,1)S(1)}, bf16[1024,512]{1,0:T(8,128)(2,1)S(1)}, u32[]{:S(2)}, u32[]{:S(2)}) %collective-permute-start.2) | collective-permute-done | bytes 1048608 | tf_op jit(solution)/shard_map/ppermute | solution.py:717
  40.9 47.8 %shard_map.306 = (bf16[1024,512]{1,0:T(8,128)(2,1)}, f32[1024,512]{1,0:T(8,128)}, bf16[1024,512]{1,0:T(8,128)(2,1)}, bf16[1024,512]{1,0:T(8,128)(2,1)}, bf16[102...) custom-call(s32[13]{0:T(128)} %get-tuple-element.58.meta_ref, ...), custom_call_target="tpu_custom_call" | custom-call | flops 32212254720 | bytes 31418420 | tf_op jit(solution)/shard_map/pallas_call | solution.py:609
  88.7 33.5 %collective-permute-start.4 = (bf16[2112,512]{1,0:T(8,128)(2,1)}, bf16[2112,512]{1,0:T(8,128)(2,1)}, u32[]{:S(2)}, u32[]{:S(2)}) collective-permute-start(bf16[2112,512]{1,0:T(8,128)(2,1)} %get-tuple-element.74), channel_id=1, source_target_pairs={{0,1},{1,0},{2,3},{3,2},{4,5},{5,4},{6,7},{7,6},{8,9},{9,8},{10,11... | collective-permute-start | bytes 6488072 | tf_op jit(solution)/shard_map/ppermute | solution.py:644
  122.2 4.2 %collective-permute-done.4 = bf16[2112,512]{1,0:T(8,128)(2,1)} collective-permute-done((bf16[2112,512]{1,0:T(8,128)(2,1)}, bf16[2112,512]{1,0:T(8,128)(2,1)}, u32[]{:S(2)}, u32[]{:S(2)}) %collective-permute-start.4) | collective-permute-done | bytes 2162720 | tf_op jit(solution)/shard_map/ppermute | solution.py:644
  126.4 2.9 %add.107 = bf16[2112,512]{1,0:T(8,128)(2,1)S(1)} add(bf16[2112,512]{1,0:T(8,128)(2,1)} %get-tuple-element.73, bf16[2112,512]{1,0:T(8,128)(2,1)} %collective-permute-done.4) | non-fusion elementwise | flops 1081344 | bytes 6488064 | tf_op jit(solution)/shard_map/add | solution.py:807
  130.3 9.8 %collective-permute-done.8 = bf16[544,512]{1,0:T(8,128)(2,1)} collective-permute-done((bf16[544,512]{1,0:T(8,128)(2,1)}, bf16[544,512]{1,0:T(8,128)(2,1)}, u32[]{:S(2)}, u32[]{:S(2)}) %collective-permute-start.8) | collective-permute-done | bytes 557088 | tf_op jit(solution)/shard_map/ppermute | solution.py:644
  144.1 6.5 %collective-permute-done.9 = bf16[512,512]{1,0:T(8,128)(2,1)S(1)} collective-permute-done((bf16[512,512]{1,0:T(8,128)(2,1)S(1)}, bf16[512,512]{1,0:T(8,128)(2,1)S(1)}, u32[]{:S(2)}, u32[]{:S(2)}) %collective-permute-start.9) | collective-permute-done | bytes 524320 | tf_op jit(solution)/shard_map/ppermute | solution.py:644
  152.2 15.4 %collective-permute-start.16 = (bf16[136,512]{1,0:T(8,128)(2,1)S(1)}, bf16[136,512]{1,0:T(8,128)(2,1)S(1)}, u32[]{:S(2)}, u32[]{:S(2)}) collective-permute-start(bf16[136,512]{1,0:T(8,128)(2,1)S(1)} %get-tuple-element.103), channel_id=1, source_target_pairs={{0,2},{1,3},{2,0},{3,1},{4,6},{5,7},{6,4},{7,5},{8,10},{9,11},{10,... | collective-permute-start | bytes 417800 | tf_op jit(solution)/shard_map/ppermute | solution.py:644
  167.7 6.2 %collective-permute-start.11 = (bf16[128,512]{1,0:T(8,128)(2,1)S(1)}, bf16[128,512]{1,0:T(8,128)(2,1)S(1)}, u32[]{:S(2)}, u32[]{:S(2)}) collective-permute-start(bf16[128,512]{1,0:T(8,128)(2,1)S(1)} %constant_dynamic-slice_fusion.3), channel_id=1, source_target_pairs={{0,2},{1,3},{2,0},{3,1},{4,6},{5,7},{6,4},{7,5},{8,10},{9,11},{10,... | collective-permute-start | bytes 393224 | tf_op jit(solution)/shard_map/ppermute | solution.py:644
  174.0 2.9 %collective-permute-done.11 = bf16[128,512]{1,0:T(8,128)(2,1)S(1)} collective-permute-done((bf16[128,512]{1,0:T(8,128)(2,1)S(1)}, bf16[128,512]{1,0:T(8,128)(2,1)S(1)}, u32[]{:S(2)}, u32[]{:S(2)}) %collective-permute-start.11) | collective-permute-done | bytes 131104 | tf_op jit(solution)/shard_map/ppermute | solution.py:644
  177.1 6.3 %collective-permute-done.17 = bf16[136,512]{1,0:T(8,128)(2,1)S(1)} collective-permute-done((bf16[136,512]{1,0:T(8,128)(2,1)S(1)}, bf16[136,512]{1,0:T(8,128)(2,1)S(1)}, u32[]{:S(2)}, u32[]{:S(2)}) %collective-permute-start.17) | collective-permute-done | bytes 139296 | tf_op jit(solution)/shard_map/ppermute | solution.py:644
  183.5 2.6 %collective-permute-done.12 = bf16[128,512]{1,0:T(8,128)(2,1)S(1)} collective-permute-done((bf16[128,512]{1,0:T(8,128)(2,1)S(1)}, bf16[128,512]{1,0:T(8,128)(2,1)S(1)}, u32[]{:S(2)}, u32[]{:S(2)}) %collective-permute-start.12) | collective-permute-done | bytes 131104 | tf_op jit(solution)/shard_map/ppermute | solution.py:644
  186.3 1.5 add.110
  189.1 2.1 collective-permute-done.13
  192.2 3.4 %collective-permute-done.19 = bf16[272,512]{1,0:T(8,128)(2,1)S(1)} collective-permute-done((bf16[272,512]{1,0:T(8,128)(2,1)S(1)}, bf16[272,512]{1,0:T(8,128)(2,1)S(1)}, u32[]{:S(2)}, u32[]{:S(2)}) %collective-permute-start.19) | collective-permute-done | bytes 278560 | tf_op jit(solution)/shard_map/ppermute | solution.py:644
  195.7 3.9 %collective-permute-start.20 = (bf16[544,512]{1,0:T(8,128)(2,1)S(1)}, bf16[544,512]{1,0:T(8,128)(2,1)S(1)}, u32[]{:S(2)}, u32[]{:S(2)}) collective-permute-start(bf16[544,512]{1,0:T(8,128)(2,1)S(1)} %constant_dynamic-update-slice_fusion.6), channel_id=1, source_target_pairs={{0,8},{1,17},{2,10},{3,19},{4,12},{5,21},{6,14},{7,23},{8,0},{9,25... | collective-permute-start | bytes 1671176 | tf_op jit(solution)/shard_map/ppermute | solution.py:644
  199.6 5.5 %collective-permute-start.22 = (bf16[512,512]{1,0:T(8,128)(2,1)S(1)}, bf16[512,512]{1,0:T(8,128)(2,1)S(1)}, u32[]{:S(2)}, u32[]{:S(2)}) collective-permute-start(bf16[512,512]{1,0:T(8,128)(2,1)S(1)} %constant_dynamic-update-slice_fusion.2), channel_id=1, source_target_pairs={{0,8},{1,17},{2,10},{3,19},{4,12},{5,21},{6,14},{7,23},{8,0},{9,25... | collective-permute-start | bytes 1572872 | tf_op jit(solution)/shard_map/ppermute | solution.py:644
  205.3 1.7 collective-permute-done.20
  207.3 5.4 %collective-permute-done.22 = bf16[512,512]{1,0:T(8,128)(2,1)S(1)} collective-permute-done((bf16[512,512]{1,0:T(8,128)(2,1)S(1)}, bf16[512,512]{1,0:T(8,128)(2,1)S(1)}, u32[]{:S(2)}, u32[]{:S(2)}) %collective-permute-start.22) | collective-permute-done | bytes 524320 | tf_op jit(solution)/shard_map/ppermute | solution.py:644
  212.8 1.9 convert_add_fusion
  215.4 3.6 %shard_map.307 = (f32[1024,512]{1,0:T(8,128)}, f32[512,1024]{1,0:T(8,128)}, f32[512,512]{1,0:T(8,128)}, f32[512,512]{1,0:T(8,128)}, f32[512,512]{1,0:T(8,128)}, ...) custom-call(s32[1]{0:T(128)} %bitcast.10.core_ref, ...), custom_call_target="tpu_custom_call" | custom-call | bytes 12734468 | tf_op jit(solution)/shard_map/pallas_call | solution.py:609
  (80 shorter events, 13.7 us)
Async XLA Ops:
  0.7 7.0 %collective-permute-start = (bf16[1024,512]{1,0:T(8,128)(2,1)}, bf16[1024,512]{1,0:T(8,128)(2,1)S(1)}, u32[]{:S(2)}, u32[]{:S(2)}) collective-permute-start(bf16[1024,512]{1,0:T(8,128)(2,1)} %refs_15_.1), channel_id=1, source_target_pairs={{0,1},{1,0},{2,3},{3,2},{4,5},{5,4},{6,7},{7,6},{8,9},{9,8},{10,11... | collective-permute-start | bytes 3145736 | tf_op jit(solution)/shard_map/ppermute | solution.py:717
  1.2 25.3 %collective-permute-start.1 = (bf16[1024,512]{1,0:T(8,128)(2,1)}, bf16[1024,512]{1,0:T(8,128)(2,1)S(1)}, u32[]{:S(2)}, u32[]{:S(2)}) collective-permute-start(bf16[1024,512]{1,0:T(8,128)(2,1)} %refs_15_.1), channel_id=1, source_target_pairs={{1,2},{3,4},{5,6},{2,1},{4,3},{6,5},{9,10},{11,12},{13,14},{10,9},... | collective-permute-start | bytes 3145736 | tf_op jit(solution)/shard_map/ppermute | solution.py:721
  1.9 35.8 %collective-permute-start.3 = (bf16[1024,512]{1,0:T(8,128)(2,1)}, bf16[1024,512]{1,0:T(8,128)(2,1)S(1)}, u32[]{:S(2)}, u32[]{:S(2)}) collective-permute-start(bf16[1024,512]{1,0:T(8,128)(2,1)} %refs_15_.1), channel_id=1, source_target_pairs={{0,2},{2,4},{4,6},{3,1},{5,3},{7,5},{8,10},{10,12},{12,14},{11,9},... | collective-permute-start | bytes 3145736 | tf_op jit(solution)/shard_map/ppermute | solution.py:725
  26.5 13.4 %collective-permute-start.2 = (bf16[1024,512]{1,0:T(8,128)(2,1)S(1)}, bf16[1024,512]{1,0:T(8,128)(2,1)S(1)}, u32[]{:S(2)}, u32[]{:S(2)}) collective-permute-start(bf16[1024,512]{1,0:T(8,128)(2,1)S(1)} %collective-permute-done.1.refs_8_), channel_id=1, source_target_pairs={{0,1},{1,0},{2,3},{3,2},{4,5},{5,4},{6,7},{7,6},{8,9},{9,8},{10,11... | collective-permute-start | bytes 3145736 | tf_op jit(solution)/shard_map/ppermute | solution.py:717
  88.7 37.7 %collective-permute-start.4 = (bf16[2112,512]{1,0:T(8,128)(2,1)}, bf16[2112,512]{1,0:T(8,128)(2,1)}, u32[]{:S(2)}, u32[]{:S(2)}) collective-permute-start(bf16[2112,512]{1,0:T(8,128)(2,1)} %get-tuple-element.74), channel_id=1, source_target_pairs={{0,1},{1,0},{2,3},{3,2},{4,5},{5,4},{6,7},{7,6},{8,9},{9,8},{10,11... | collective-permute-start | bytes 6488072 | tf_op jit(solution)/shard_map/ppermute | solution.py:644
  130.2 9.8 %collective-permute-start.8 = (bf16[544,512]{1,0:T(8,128)(2,1)}, bf16[544,512]{1,0:T(8,128)(2,1)}, u32[]{:S(2)}, u32[]{:S(2)}) collective-permute-start(bf16[544,512]{1,0:T(8,128)(2,1)} %constant_dynamic-slice_fusion.6), channel_id=1, source_target_pairs={{0,8},{1,17},{2,10},{3,19},{4,12},{5,21},{6,14},{7,23},{8,0},{9,25... | collective-permute-start | bytes 1671176 | tf_op jit(solution)/shard_map/ppermute | solution.py:644
  141.3 9.2 %collective-permute-start.9 = (bf16[512,512]{1,0:T(8,128)(2,1)S(1)}, bf16[512,512]{1,0:T(8,128)(2,1)S(1)}, u32[]{:S(2)}, u32[]{:S(2)}) collective-permute-start(bf16[512,512]{1,0:T(8,128)(2,1)S(1)} %constant_dynamic-slice_fusion.5), channel_id=1, source_target_pairs={{0,8},{1,17},{2,10},{3,19},{4,12},{5,21},{6,14},{7,23},{8,0},{9,25... | collective-permute-start | bytes 1572872 | tf_op jit(solution)/shard_map/ppermute | solution.py:644
  141.5 44.8 %collective-permute-start.7 = (bf16[1024,512]{1,0:T(8,128)(2,1)}, bf16[1024,512]{1,0:T(8,128)(2,1)}, u32[]{:S(2)}, u32[]{:S(2)}) collective-permute-start(bf16[1024,512]{1,0:T(8,128)(2,1)} %get-tuple-element.79), channel_id=1, source_target_pairs={{0,1},{1,0},{2,3},{3,2},{4,5},{5,4},{6,7},{7,6},{8,9},{9,8},{10,11... | collective-permute-start | bytes 3145736 | tf_op jit(solution)/shard_map/ppermute | solution.py:717
  141.6 32.3 %collective-permute-start.6 = (bf16[1024,512]{1,0:T(8,128)(2,1)}, bf16[1024,512]{1,0:T(8,128)(2,1)S(1)}, u32[]{:S(2)}, u32[]{:S(2)}) collective-permute-start(bf16[1024,512]{1,0:T(8,128)(2,1)} %get-tuple-element.77), channel_id=1, source_target_pairs={{2,0},{4,2},{6,4},{1,3},{3,5},{5,7},{10,8},{12,10},{14,12},{9,11},... | collective-permute-start | bytes 3145736 | tf_op jit(solution)/shard_map/ppermute | solution.py:725
  142.9 9.2 %collective-permute-start.15 = (bf16[272,512]{1,0:T(8,128)(2,1)S(1)}, bf16[272,512]{1,0:T(8,128)(2,1)S(1)}, u32[]{:S(2)}, u32[]{:S(2)}) collective-permute-start(bf16[272,512]{1,0:T(8,128)(2,1)S(1)} %constant_dynamic-slice_fusion.2), channel_id=1, source_target_pairs={{0,16},{1,9},{2,18},{3,11},{4,20},{5,13},{6,22},{7,15},{8,24},{9,1... | collective-permute-start | bytes 835592 | tf_op jit(solution)/shard_map/ppermute | solution.py:644
  151.8 15.8 %collective-permute-start.10 = (bf16[256,512]{1,0:T(8,128)(2,1)S(1)}, bf16[256,512]{1,0:T(8,128)(2,1)S(1)}, u32[]{:S(2)}, u32[]{:S(2)}) collective-permute-start(bf16[256,512]{1,0:T(8,128)(2,1)S(1)} %constant_dynamic-slice_fusion.4), channel_id=1, source_target_pairs={{0,16},{1,9},{2,18},{3,11},{4,20},{5,13},{6,22},{7,15},{8,24},{9,1... | collective-permute-start | bytes 786440 | tf_op jit(solution)/shard_map/ppermute | solution.py:644
  152.2 21.7 %collective-permute-start.16 = (bf16[136,512]{1,0:T(8,128)(2,1)S(1)}, bf16[136,512]{1,0:T(8,128)(2,1)S(1)}, u32[]{:S(2)}, u32[]{:S(2)}) collective-permute-start(bf16[136,512]{1,0:T(8,128)(2,1)S(1)} %get-tuple-element.103), channel_id=1, source_target_pairs={{0,2},{1,3},{2,0},{3,1},{4,6},{5,7},{6,4},{7,5},{8,10},{9,11},{10,... | collective-permute-start | bytes 417800 | tf_op jit(solution)/shard_map/ppermute | solution.py:644
  167.7 9.3 %collective-permute-start.11 = (bf16[128,512]{1,0:T(8,128)(2,1)S(1)}, bf16[128,512]{1,0:T(8,128)(2,1)S(1)}, u32[]{:S(2)}, u32[]{:S(2)}) collective-permute-start(bf16[128,512]{1,0:T(8,128)(2,1)S(1)} %constant_dynamic-slice_fusion.3), channel_id=1, source_target_pairs={{0,2},{1,3},{2,0},{3,1},{4,6},{5,7},{6,4},{7,5},{8,10},{9,11},{10,... | collective-permute-start | bytes 393224 | tf_op jit(solution)/shard_map/ppermute | solution.py:644
  174.0 9.4 %collective-permute-start.17 = (bf16[136,512]{1,0:T(8,128)(2,1)S(1)}, bf16[136,512]{1,0:T(8,128)(2,1)S(1)}, u32[]{:S(2)}, u32[]{:S(2)}) collective-permute-start(bf16[136,512]{1,0:T(8,128)(2,1)S(1)} %add.135), channel_id=1, source_target_pairs={{0,4},{1,5},{2,6},{3,7},{4,0},{5,1},{6,2},{7,3},{8,12},{9,13},{10,... | collective-permute-start | bytes 417800 | tf_op jit(solution)/shard_map/ppermute | solution.py:644
  177.0 9.1 %collective-permute-start.12 = (bf16[128,512]{1,0:T(8,128)(2,1)S(1)}, bf16[128,512]{1,0:T(8,128)(2,1)S(1)}, u32[]{:S(2)}, u32[]{:S(2)}) collective-permute-start(bf16[128,512]{1,0:T(8,128)(2,1)S(1)} %dynamic-slice_add_fusion.4), channel_id=1, source_target_pairs={{0,4},{1,5},{2,6},{3,7},{4,0},{5,1},{6,2},{7,3},{8,12},{9,13},{10,... | collective-permute-start | bytes 393224 | tf_op jit(solution)/shard_map/ppermute | solution.py:644
  183.4 5.6 %collective-permute-start.18 = (bf16[136,512]{1,0:T(8,128)(2,1)S(1)}, bf16[136,512]{1,0:T(8,128)(2,1)S(1)}, u32[]{:S(2)}, u32[]{:S(2)}) collective-permute-start(bf16[136,512]{1,0:T(8,128)(2,1)S(1)} %get-tuple-element.100), channel_id=1, source_target_pairs={{0,2},{1,3},{2,0},{3,1},{4,6},{5,7},{6,4},{7,5},{8,10},{9,11},{10,... | collective-permute-start | bytes 417800 | tf_op jit(solution)/shard_map/ppermute | solution.py:644
  186.2 5.0 %collective-permute-start.13 = (bf16[128,512]{1,0:T(8,128)(2,1)S(1)}, bf16[128,512]{1,0:T(8,128)(2,1)S(1)}, u32[]{:S(2)}, u32[]{:S(2)}) collective-permute-start(bf16[128,512]{1,0:T(8,128)(2,1)S(1)} %get-tuple-element.102), channel_id=1, source_target_pairs={{0,2},{1,3},{2,0},{3,1},{4,6},{5,7},{6,4},{7,5},{8,10},{9,11},{10,... | collective-permute-start | bytes 393224 | tf_op jit(solution)/shard_map/ppermute | solution.py:644
  189.0 6.6 %collective-permute-start.19 = (bf16[272,512]{1,0:T(8,128)(2,1)S(1)}, bf16[272,512]{1,0:T(8,128)(2,1)S(1)}, u32[]{:S(2)}, u32[]{:S(2)}) collective-permute-start(bf16[272,512]{1,0:T(8,128)(2,1)S(1)} %constant_dynamic-update-slice_fusion.8), channel_id=1, source_target_pairs={{0,16},{1,9},{2,18},{3,11},{4,20},{5,13},{6,22},{7,15},{8,24},{9,1... | collective-permute-start | bytes 835592 | tf_op jit(solution)/shard_map/ppermute | solution.py:644
  191.3 15.9 %collective-permute-start.14 = (bf16[1024,512]{1,0:T(8,128)(2,1)S(1)}, bf16[1024,512]{1,0:T(8,128)(2,1)S(1)}, u32[]{:S(2)}, u32[]{:S(2)}) collective-permute-start(bf16[1024,512]{1,0:T(8,128)(2,1)S(1)} %add.110), channel_id=1, source_target_pairs={{1,2},{3,4},{5,6},{2,1},{4,3},{6,5},{9,10},{11,12},{13,14},{10,9},... | collective-permute-start | bytes 3145736 | tf_op jit(solution)/shard_map/ppermute | solution.py:721
  192.1 7.5 %collective-permute-start.21 = (bf16[256,512]{1,0:T(8,128)(2,1)S(1)}, bf16[256,512]{1,0:T(8,128)(2,1)S(1)}, u32[]{:S(2)}, u32[]{:S(2)}) collective-permute-start(bf16[256,512]{1,0:T(8,128)(2,1)S(1)} %constant_dynamic-update-slice_fusion.10), channel_id=1, source_target_pairs={{0,16},{1,9},{2,18},{3,11},{4,20},{5,13},{6,22},{7,15},{8,24},{9,1... | collective-permute-start | bytes 786440 | tf_op jit(solution)/shard_map/ppermute | solution.py:644
  195.7 11.4 %collective-permute-start.20 = (bf16[544,512]{1,0:T(8,128)(2,1)S(1)}, bf16[544,512]{1,0:T(8,128)(2,1)S(1)}, u32[]{:S(2)}, u32[]{:S(2)}) collective-permute-start(bf16[544,512]{1,0:T(8,128)(2,1)S(1)} %constant_dynamic-update-slice_fusion.6), channel_id=1, source_target_pairs={{0,8},{1,17},{2,10},{3,19},{4,12},{5,21},{6,14},{7,23},{8,0},{9,25... | collective-permute-start | bytes 1671176 | tf_op jit(solution)/shard_map/ppermute | solution.py:644
  199.6 13.0 %collective-permute-start.22 = (bf16[512,512]{1,0:T(8,128)(2,1)S(1)}, bf16[512,512]{1,0:T(8,128)(2,1)S(1)}, u32[]{:S(2)}, u32[]{:S(2)}) collective-permute-start(bf16[512,512]{1,0:T(8,128)(2,1)S(1)} %constant_dynamic-update-slice_fusion.2), channel_id=1, source_target_pairs={{0,8},{1,17},{2,10},{3,19},{4,12},{5,21},{6,14},{7,23},{8,0},{9,25... | collective-permute-start | bytes 1572872 | tf_op jit(solution)/shard_map/ppermute | solution.py:644
  205.1 7.6 %collective-permute-start.5 = (bf16[1024,512]{1,0:T(8,128)(2,1)S(1)}, bf16[1024,512]{1,0:T(8,128)(2,1)S(1)}, u32[]{:S(2)}, u32[]{:S(2)}) collective-permute-start(bf16[1024,512]{1,0:T(8,128)(2,1)S(1)} %copy-done.3), channel_id=1, source_target_pairs={{0,1},{1,0},{2,3},{3,2},{4,5},{5,4},{6,7},{7,6},{8,9},{9,8},{10,11... | collective-permute-start | bytes 3145736 | tf_op jit(solution)/shard_map/ppermute | solution.py:717
  207.1 7.6 %collective-permute-start.23 = (bf16[1088,512]{1,0:T(8,128)(2,1)S(1)}, bf16[1088,512]{1,0:T(8,128)(2,1)S(1)}, u32[]{:S(2)}, u32[]{:S(2)}) collective-permute-start(bf16[1088,512]{1,0:T(8,128)(2,1)S(1)} %constant_dynamic-update-slice_fusion.4.mine_one), channel_id=1, source_target_pairs={{0,1},{1,0},{2,3},{3,2},{4,5},{5,4},{6,7},{7,6},{8,9},{9,8},{10,11... | collective-permute-start | bytes 3342344 | tf_op jit(solution)/shard_map/ppermute | solution.py:644
  (9 other events, 90.3 us)
